TPU v7x, 256 devices: a whole 4x4x8 slice. The times are simulated.
256 devices in a mesh: tok: 8 (over y, core), lat: 32 (over z, x).
Axes of the slice: x: 4, y: 4, z: 8, core: 2. Of those that a mesh axis runs over, the one named last changes fastest.
Arguments:
- tokens: bfloat16 [32768, 8192], P(('tok', 'lat')), may hold values from -6 to 6
- dec_bias: float32 [8192], replicated, may hold values from -3 to 3
- enc_weight: bfloat16 [4096, 8192], P('lat'), may hold values from -0.0625 to 0.0625
- enc_bias: float32 [4096], P('lat'), may hold values from -3 to 3
- dec_weight: bfloat16 [4096, 8192], P('lat'), may hold values from -0.75 to 0.75
- block_ids: int32 [32768, 1], P(('tok', 'lat')), may hold values from 0 to 63, as said below
- block_home: int32 [64], replicated, may hold values from 0 to 63, as said below
Outputs:
- enc_grad: float32 [4096, 8192], P('lat', 'tok')
- dec_grad: float32 [4096, 8192], P('lat', 'tok')
Inputs may be any that keep to these rules, and one draw needn't show every extreme that they name: `block_ids`: each row names 1 different blocks. The 128 names in the rows of one device (aligned groups of 128 rows) name each block at most 6 times; in every token group the blocks of one lat device are each named exactly 6 times by the rows of every device of the group. A permutation: block b has place block_home[b], held by lat device block_home[b] // 2.
All inputs are finite; a program needn't handle non-finite values.
Results may differ from a plain program's by a relative error of at most 0.0024.
Values may be sent and summed in bfloat16 or wider, within the bound.
No kernel may reach another device: no remote copies, remote signals or barrier semaphores. Data moves between devices by JAX's collectives and lax.ppermute only.
A program may use at most 128 MiB of HBM per device.

v0:
```python
import functools

import jax
import jax.numpy as jnp
from jax import lax
from jax.experimental import pallas as pl
from jax.experimental.pallas import tpu as pltpu
from jax.sharding import PartitionSpec as P

BF = jnp.bfloat16
F32 = jnp.float32
I32 = jnp.int32

CUTS = 4
SLOTS = 2
DIRECT = 2 * SLOTS
GROUP = CUTS * SLOTS
STRIDE = 8
EMPTY = 2.0**100
STEP = 1024
PIECES = 8
LENT = (6, 7)


def room(mib):
    return pltpu.CompilerParams(vmem_limit_bytes=mib * 2**20)


def mm(a, b):
    return jnp.dot(a, b, preferred_element_type=F32)


def mm_t(a, b):
    return lax.dot_general(a, b, (((1,), (1,)), ((), ())), preferred_element_type=F32)


def iota(shape, axis):
    return lax.broadcasted_iota(I32, shape, axis)


def flat(mask):
    return jnp.where(mask, 1.0, 0.0)


def slot_codes(targets, first):
    row = iota((targets * GROUP, 1), 0)
    inner = row % GROUP
    return (row // GROUP) * STRIDE + first + inner % SLOTS, inner // SLOTS


def before(n):
    return (iota((n, n), 0) < iota((n, n), 1)).astype(F32).astype(BF)


def ranks_of(target, targets):
    g, n = target.shape
    members = flat(target[:, None, :] == iota((g, targets, n), 1))
    counts = mm(members.reshape(g * targets, n).astype(BF), before(n)).reshape(g, targets, n)
    return members, jnp.sum(members * counts, axis=1)


def target_of(places, targets):
    return (places & 1) * (targets // 2) + (places >> 1)


def cut_columns(ref, i):
    part = ref.shape[1] // CUTS
    return [ref[:, h * part + i * STEP : h * part + (i + 1) * STEP] for h in range(CUTS)]


def first_kernel(targets, ids, home, tokens, chunk, lent_a, lent_b):
    rows, width = tokens.shape
    part = width // CUTS
    total = home.shape[1]
    named = flat(iota((total, rows), 0) == ids[...]).astype(BF)
    table = jnp.broadcast_to(home[...], (8, total)).astype(F32).astype(BF)
    places = mm(table, named)[:1].astype(I32)
    target = target_of(places, targets)
    unused, rank = ranks_of(target, targets)
    rank = rank.astype(I32)
    codes, cut = slot_codes(targets, 0)
    hit = flat(codes == target * STRIDE + rank)
    wide = jnp.concatenate([jnp.where(cut == h, hit, 0.0) for h in range(CUTS)], axis=1)
    wide = wide.astype(BF)
    filled = jnp.sum(hit, axis=1, keepdims=True) > 0.5
    for i in range(part // STEP):
        got = mm(wide, jnp.concatenate(cut_columns(tokens, i), axis=0))
        chunk[:, i * STEP : (i + 1) * STEP] = jnp.where(filled, got, EMPTY).astype(BF)
    over = flat(rank >= DIRECT)
    order = mm(jnp.broadcast_to(over, (8, rows)).astype(BF), before(rows))[:1].astype(I32)
    first = 0
    for count, lent in zip(LENT, (lent_a, lent_b)):
        lines = lent.shape[0]
        line = iota((lines, rows), 0)
        take = jnp.logical_and(order == first + line // PIECES, over > 0.5)
        take = flat(jnp.logical_and(take, line < count * PIECES))
        piece = iota((lines, 1), 0) % PIECES
        got = jnp.zeros((lines, STEP), F32)
        for i in range(PIECES):
            chosen = jnp.where(piece == i, take, 0.0).astype(BF)
            got = got + mm(chosen, tokens[:, i * STEP : (i + 1) * STEP])
        if first == 0:
            head = jnp.where(line == count * PIECES, places.astype(F32), got[:, :rows])
            got = jnp.concatenate([head, got[:, rows:]], axis=1)
        lent[...] = got.astype(BF)
        first += count


def second_kernel(targets, group, tokens, loans_a, loans_b, chunk, left, flags):
    rows, width = tokens.shape
    part = width // CUTS
    lines = (LENT[0] + 1) * PIECES
    groups = loans_a.shape[0] // lines
    me = group[0]
    heads = loans_a[:, :rows].astype(F32).reshape(groups, lines, rows)
    places = heads[:, LENT[0] * PIECES, :].astype(I32)
    target = target_of(places, targets)
    members, rank_f = ranks_of(target, targets)
    rank = rank_f.astype(I32)
    over = rank >= DIRECT
    order = mm(flat(over).astype(BF), before(rows)).astype(I32)
    listed = jnp.logical_and(over, order < sum(LENT))
    count = jnp.sum(members, axis=2, keepdims=True)
    asked = jnp.sum(members * flat(listed)[:, None, :], axis=2, keepdims=True)
    used = jnp.maximum(count, float(SLOTS))
    free = jnp.maximum(DIRECT - used, 0.0)
    asked_before = []
    running = jnp.zeros((1, targets, 1), F32)
    free_total = jnp.zeros((1, targets, 1), F32)
    free_before = jnp.zeros((1, targets, 1), F32)
    for t in range(groups):
        asked_before.append(running)
        running = running + asked[t : t + 1]
        free_before = free_before + jnp.where(me > t, free[t : t + 1], 0.0)
        free_total = free_total + free[t : t + 1]
    mine = flat(iota((groups, 1, 1), 0) == me)
    my_free = jnp.sum(free * mine, axis=0, keepdims=True)
    my_used = jnp.sum(used * mine, axis=0, keepdims=True)

    def look(values):
        return jnp.sum(members * values, axis=1).astype(I32)

    in_pool = look(jnp.concatenate(asked_before, axis=0)) + rank - DIRECT
    placed = jnp.logical_and(listed, in_pool < look(free_total))
    at = in_pool - look(free_before)
    here = jnp.logical_and(placed, jnp.logical_and(at >= 0, at < look(my_free)))
    lent_code = jnp.where(here, target * STRIDE + look(my_used) + at, -1)
    size = groups * lines
    square = iota((size, size), 0) == iota((size, size), 1)
    line_of = iota((lines, rows), 0) // PIECES

    def codes_of_lines(first, count):
        columns = []
        for t in range(groups):
            chosen = jnp.logical_and(order[t : t + 1] == first + line_of, listed[t : t + 1])
            chosen = jnp.logical_and(chosen, line_of < count)
            value = jnp.where(chosen, lent_code[t : t + 1] + 1, 0)
            columns.append(jnp.sum(value, axis=1, keepdims=True) - 1)
        column = jnp.concatenate(columns, axis=0)
        return jnp.sum(jnp.where(square, column, 0), axis=0, keepdims=True)

    mine2 = (iota((groups, 1), 0) == me).astype(I32)
    own_code = jnp.sum((target * STRIDE + rank) * mine2, axis=0, keepdims=True)
    missing = jnp.logical_and(over, jnp.logical_not(placed)).astype(I32)
    own_missing = jnp.sum(missing * mine2, axis=0, keepdims=True)
    left[...] = jnp.broadcast_to(jnp.where(own_missing > 0, own_code, -1), left.shape)
    flag = jnp.max(jnp.max(missing.astype(F32), axis=1, keepdims=True), axis=0, keepdims=True)
    codes, cut = slot_codes(targets, SLOTS)
    hit = flat(codes == own_code)
    wide = jnp.concatenate([jnp.where(cut == h, hit, 0.0) for h in range(CUTS)], axis=1)
    wide = wide.astype(BF)
    hit_a = flat(codes == codes_of_lines(0, LENT[0]))
    hit_b = flat(codes == codes_of_lines(LENT[0], LENT[1]))
    filled = jnp.sum(hit, axis=1, keepdims=True) + jnp.sum(hit_a, axis=1, keepdims=True)
    filled = filled + jnp.sum(hit_b, axis=1, keepdims=True) > 0.5
    flags[...] = jnp.broadcast_to(flag, flags.shape)
    per_cut = part // STEP
    piece = iota((1, size), 1) % PIECES
    for i in range(per_cut):
        at_cut = cut * per_cut + i == piece
        got = mm(wide, jnp.concatenate(cut_columns(tokens, i), axis=0))
        got = got + mm(jnp.where(at_cut, hit_a, 0.0).astype(BF), loans_a[...])
        got = got + mm(jnp.where(at_cut, hit_b, 0.0).astype(BF), loans_b[...])
        chunk[:, i * STEP : (i + 1) * STEP] = jnp.where(filled, got, EMPTY).astype(BF)


def gradient_body(chunk, enc, dec, bias, dec_bias, cent, err, acc, store, ready):
    rows, part = chunk.shape
    latents = enc.shape[0]
    steps = part // STEP
    inner = iota((rows, 1), 0) % GROUP
    cut = inner // SLOTS
    cut8 = iota((GROUP, 1), 0) // SLOTS

    def here(i):
        return slice(i * STEP, (i + 1) * STEP)

    def offset(i):
        value = jnp.zeros((GROUP, STEP), F32)
        for h, columns in enumerate(cut_columns(dec_bias, i)):
            value = jnp.where(cut8 == h, columns, value)
        return value[None]

    def joined(total):
        own = total[:, :latents]
        for h in range(1, CUTS):
            own = jnp.where(cut == h, total[:, h * latents : (h + 1) * latents], own)
        shift = GROUP // 2
        while shift >= SLOTS:
            down = pltpu.roll(own, rows - shift, 0)
            wrapped = pltpu.roll(own, GROUP - shift, 0)
            own = own + jnp.where(inner < GROUP - shift, down, wrapped)
            shift //= 2
        return own

    def spread(values):
        return jnp.concatenate([jnp.where(cut == h, values, 0.0) for h in range(CUTS)], axis=1)

    for i in range(steps):
        ready("first", i)
        x = chunk[:, here(i)].astype(F32).reshape(rows // GROUP, GROUP, STEP)
        c = (x - offset(i)).reshape(rows, STEP).astype(BF)
        cent[:, here(i)] = c
        w = jnp.concatenate(cut_columns(enc, i), axis=0)
        if i == 0:
            acc[...] = mm_t(c, w)
        else:
            acc[...] += mm_t(c, w)
    valid = chunk[:, :latents].astype(F32) < EMPTY / 2
    pre = joined(acc[...]) + bias[...]
    gate = 1.0 / (1.0 + jnp.exp(-pre))
    latent = spread(jnp.where(valid, pre * gate, 0.0))
    latent_b = latent.astype(BF)
    ready("second", 0)
    for i in range(steps):
        w = jnp.concatenate(cut_columns(dec, i), axis=0)
        d = mm(latent_b, w).astype(BF).astype(F32).reshape(rows // GROUP, GROUP, STEP)
        x = chunk[:, here(i)].astype(F32).reshape(rows // GROUP, GROUP, STEP)
        e = ((offset(i) + d - x) * (1.0 / 32.0)).reshape(rows, STEP).astype(BF)
        err[:, here(i)] = e
        if i == 0:
            acc[...] = mm_t(e, w)
        else:
            acc[...] += mm_t(e, w)
    dlatent = joined(acc[...])
    dpre = spread(jnp.where(valid, dlatent * gate * (1.0 + pre * (1.0 - gate)), 0.0))
    dpre_t = dpre.T.astype(BF)
    latent_t = latent.T.astype(BF)
    ready("third", 0)
    for i in range(steps):
        store(i, 0, mm(dpre_t, cent[:, here(i)]))
        store(i, 1, mm(latent_t, err[:, here(i)]))


class Loader:
    def __init__(self, sems, first_row, chunk_in, enc_in, dec_in, chunk, enc, dec):
        self.sems = sems
        self.moves = {}
        part = chunk.shape[1]
        latents = enc.shape[0]
        rows = pl.ds(pl.multiple_of(first_row, latents), latents)
        for i in range(part // STEP):
            here = pl.ds(i * STEP, STEP)
            self.move(("chunk", i), chunk_in.at[:, here], chunk.at[:, here])
            for h in range(CUTS):
                columns = pl.ds(h * part + i * STEP, STEP)
                self.move(("enc", i, h), enc_in.at[rows, columns], enc.at[:, columns])
        self.move("second", dec_in.at[rows], dec)

    def move(self, key, source, target):
        self.moves[key] = pltpu.make_async_copy(source, target, self.sems.at[len(self.moves)])
        self.moves[key].start()

    def __call__(self, stage, i):
        if stage == "first":
            self.moves[("chunk", i)].wait()
            for h in range(CUTS):
                self.moves[("enc", i, h)].wait()
        elif stage in self.moves:
            self.moves[stage].wait()


def part_kernel(
    at, chunk_in, enc_in, dec_in, bias, dec_bias, parts, chunk, enc, dec, cent, err, acc, sems
):
    latents = enc.shape[0]
    ready = Loader(sems, at[1], chunk_in, enc_in, dec_in, chunk, enc, dec)

    def store(i, grad, value):
        rows = slice(grad * latents, (grad + 1) * latents)
        for h in range(CUTS):
            parts[i, h, rows] = value[h * latents : (h + 1) * latents]

    gradient_body(chunk, enc, dec, bias, dec_bias, cent, err, acc, store, ready)


def last_kernel(
    at,
    chunk_in,
    enc_in,
    dec_in,
    bias,
    dec_bias,
    parts_in,
    mine_out,
    other_out,
    chunk,
    enc,
    dec,
    cent,
    err,
    acc,
    sems,
    parts,
    mine,
    other,
    sems_out,
):
    latents = enc.shape[0]
    core = at[0]
    ready = Loader(sems, at[1], chunk_in, enc_in, dec_in, chunk, enc, dec)
    ready.move("third", parts_in, parts)

    def out_copy(which, grad):
        source, result = ((mine, mine_out), (other, other_out))[which]
        rows = pl.ds(grad * latents, latents)
        sem = sems_out.at[2 * which + grad]
        return pltpu.make_async_copy(source.at[:, rows], result.at[:, rows], sem)

    def store(i, grad, value):
        rows = slice(grad * latents, (grad + 1) * latents)
        totals = [
            value[h * latents : (h + 1) * latents] + parts[i, h, rows] for h in range(CUTS)
        ]

        @pl.when(core == i)
        def _():
            for h in range(CUTS):
                mine[h, rows] = totals[h]
            out_copy(0, grad).start()

        @pl.when(core != i)
        def _():
            for h in range(CUTS):
                other[h, rows] = totals[h].astype(BF)
            out_copy(1, grad).start()

    gradient_body(chunk, enc, dec, bias, dec_bias, cent, err, acc, store, ready)
    for which in range(2):
        for grad in range(2):
            out_copy(which, grad).wait()


def vmem():
    return pl.BlockSpec(memory_space=pltpu.VMEM)


def anywhere():
    return pl.BlockSpec(memory_space=pl.ANY)


def smem():
    return pl.BlockSpec(memory_space=pltpu.SMEM)


def on_device(tokens, dec_bias, enc_weight, enc_bias, dec_weight, block_ids, block_home):
    rows, width = tokens.shape
    lat_count = lax.axis_size("lat")
    groups = lax.axis_size("tok")
    chips = groups // 2
    targets = 2 * lat_count
    part = width // CUTS
    slot_rows = targets * GROUP
    latents = enc_weight.shape[0] // 2
    per_cut = part // STEP
    me = lax.axis_index("tok").astype(I32)
    core = me % 2
    first_row = (me // 2 % 2) * latents
    scalars = jnp.stack([core, first_row])
    exchange_groups = [
        [(4 * p + 2 * b + c) * lat_count + at for b in range(2) for at in range(lat_count)]
        for p in range(groups // 4)
        for c in range(2)
    ]
    chunk_shape = jax.ShapeDtypeStruct((slot_rows, part), BF)
    lent_shape = jax.ShapeDtypeStruct((max(LENT) * PIECES, STEP), BF)
    matmul_cost = pl.CostEstimate(
        flops=5 * 2 * slot_rows * CUTS * latents * part,
        bytes_accessed=12 * 2**20,
        transcendentals=0,
    )
    move_cost = pl.CostEstimate(
        flops=2 * slot_rows * CUTS * rows * part, bytes_accessed=5 * 2**20, transcendentals=0
    )

    chunk1, lent_a, lent_b = pl.pallas_call(
        functools.partial(first_kernel, targets),
        out_shape=[chunk_shape, lent_shape, lent_shape],
        in_specs=[vmem()] * 3,
        out_specs=[vmem()] * 3,
        compiler_params=room(20),
        cost_estimate=move_cost,
        name="first_slots",
    )(block_ids.reshape(1, rows), block_home.reshape(1, -1), tokens)

    def exchange(chunk):
        shaped = chunk.reshape(targets, GROUP, part)
        got = lax.all_to_all(
            shaped,
            ("tok", "lat"),
            split_axis=0,
            concat_axis=0,
            tiled=True,
            axis_index_groups=exchange_groups,
        )
        return got.reshape(slot_rows, part)

    loans_a = lax.all_gather(lent_a, "tok", tiled=True)
    loans_a, lent_b = lax.optimization_barrier((loans_a, lent_b))
    loans_b = lax.all_gather(lent_b, "tok", tiled=True)
    got1 = exchange(chunk1)
    chunk2, left, flags = pl.pallas_call(
        functools.partial(second_kernel, targets),
        out_shape=[
            chunk_shape,
            jax.ShapeDtypeStruct((8, rows), I32),
            jax.ShapeDtypeStruct((8, rows), F32),
        ],
        in_specs=[smem()] + [vmem()] * 3,
        out_specs=[vmem()] * 3,
        compiler_params=room(24),
        cost_estimate=move_cost,
        name="second_slots",
    )(me.reshape(1), tokens, loans_a, loans_b)
    got2 = exchange(chunk2)
    line = 4
    along_x = [[i * line + j for j in range(line)] for i in range(lat_count // line)]
    along_z = [[i * line + j for i in range(lat_count // line)] for j in range(line)]
    for lines in (along_x, along_z):
        flags = lax.all_gather(flags, "lat", axis_index_groups=lines)
        flags = jnp.max(flags, axis=0)

    bias_row = lax.dynamic_slice_in_dim(enc_bias, first_row, latents).reshape(1, latents)
    offset_row = dec_bias.reshape(1, width)
    work = [
        pltpu.VMEM((slot_rows, part), BF),
        pltpu.VMEM((latents, width), BF),
        pltpu.VMEM((latents, width), BF),
        pltpu.VMEM((slot_rows, part), BF),
        pltpu.VMEM((slot_rows, part), BF),
        pltpu.VMEM((slot_rows, CUTS * latents), F32),
        pltpu.SemaphoreType.DMA((per_cut * (CUTS + 1) + 2,)),
    ]
    parts_shape = (per_cut, CUTS, 2 * latents, STEP)
    half_shape = (CUTS, 2 * latents, STEP)
    part_call = pl.pallas_call(
        part_kernel,
        out_shape=jax.ShapeDtypeStruct(parts_shape, F32),
        in_specs=[smem()] + [anywhere()] * 3 + [vmem()] * 2,
        out_specs=vmem(),
        scratch_shapes=work,
        compiler_params=room(56),
        cost_estimate=matmul_cost,
        name="chunk_gradients",
    )
    parts = part_call(scalars, got1, enc_weight, dec_weight, bias_row, offset_row)
    mine, other = pl.pallas_call(
        last_kernel,
        out_shape=[
            jax.ShapeDtypeStruct(half_shape, F32),
            jax.ShapeDtypeStruct(half_shape, BF),
        ],
        in_specs=[smem()] + [anywhere()] * 3 + [vmem()] * 2 + [anywhere()],
        out_specs=[anywhere()] * 2,
        scratch_shapes=[
            *work,
            pltpu.VMEM(parts_shape, F32),
            pltpu.VMEM(half_shape, F32),
            pltpu.VMEM(half_shape, BF),
            pltpu.SemaphoreType.DMA((4,)),
        ],
        compiler_params=room(56),
        cost_estimate=matmul_cost,
        name="last_gradients",
    )(scalars, got2, enc_weight, dec_weight, bias_row, offset_row, parts)

    def rest(carry):
        mine, other, unused = carry
        codes, cut = slot_codes(targets, DIRECT)
        hit = flat(codes == left[:1])
        data = jnp.zeros((slot_rows, part), F32)
        for h in range(CUTS):
            chosen = jnp.where(cut == h, hit, 0.0).astype(BF)
            data = data + mm(chosen, tokens[:, h * part : (h + 1) * part])
        filled = jnp.sum(hit, axis=1, keepdims=True) > 0.5
        chunk3 = jnp.where(filled, data, EMPTY).astype(BF)
        more = part_call(scalars, exchange(chunk3), enc_weight, dec_weight, bias_row, offset_row)
        mine = mine + lax.dynamic_index_in_dim(more, core, 0, keepdims=False)
        more = lax.dynamic_index_in_dim(more, 1 - core, 0, keepdims=False)
        return mine, (other.astype(F32) + more).astype(BF), jnp.zeros((), F32)

    mine, other, unused = lax.while_loop(
        lambda carry: carry[2] > 0.5, rest, (mine, other, flags[0, 0])
    )
    swapped = lax.ppermute(other, "tok", [(i, i ^ 1) for i in range(groups)])
    summed = (mine + swapped.astype(F32)).astype(BF)
    terms = lax.all_to_all(
        summed,
        "tok",
        split_axis=0,
        concat_axis=0,
        tiled=True,
        axis_index_groups=[[2 * i + c for i in range(chips)] for c in range(2)],
    )
    total = jnp.sum(terms.astype(F32).reshape(chips // 2, 2, 2, latents, STEP), axis=0)
    return total[:, 0].reshape(2 * latents, STEP), total[:, 1].reshape(2 * latents, STEP)


def solution(mesh):
    in_specs = (
        P(("tok", "lat"), None),
        P(),
        P("lat", None),
        P("lat"),
        P("lat", None),
        P(("tok", "lat"), None),
        P(),
    )
    out_specs = (P("lat", "tok"), P("lat", "tok"))
    return jax.shard_map(
        on_device, mesh=mesh, in_specs=in_specs, out_specs=out_specs, check_vma=False
    )
```

profile of v0, /device:TPU:6, one launch (start us, length us, event | category | flops | bytes accessed | tf_op | source)
XLA Modules:
  0.0 189.3 jit_solution(17277465506504965879)
XLA Ops:
  0.6 0.0 copy-start
  0.6 0.0 copy-start.1
  0.7 0.7 copy-done.1
  1.3 0.0 copy-start.2
  1.3 0.7 copy-done.2
  2.0 4.9 %first_slots.1 = (bf16[512,2048]{1,0:T(8,128)(2,1)}, bf16[56,1024]{1,0:T(8,128)(2,1)S(1)}, bf16[56,1024]{1,0:T(8,128)(2,1)S(1)}) custom-call(s32[1,128]{1,0:T(1,128)S(1)} %bitcast.32, s32[1,64]{1,0:T(1,128)S(1)} %bitcast.33, bf16[128,8192]{1,0:T(8,128)(2,1)} %tokens.3), custom_call_target="tpu_custom_call" | custom-call | flops 1073741824 | bytes 5242880 | tf_op jit(solution)/shard_map/first_slots/pallas_call | solution.py:396
  6.8 13.2 %all-to-all-start.2 = ((bf16[64,8,2048]{2,1,0:T(8,128)(2,1)}), bf16[64,8,2048]{2,1,0:T(8,128)(2,1)}, u32[]{:S(2)}, u32[]{:S(2)}) async-start(bf16[64,8,2048]{2,1,0:T(8,128)(2,1)} %bitcast.14), calls=%async_computation.2 | async-start | bytes 4194304 | tf_op jit(solution)/shard_map/all_to_all | solution.py:408
  20.0 16.5 %all_gather.18.loans_a = bf16[448,1024]{1,0:T(8,128)(2,1)S(1)} all-gather(bf16[56,1024]{1,0:T(8,128)(2,1)S(1)} %get-tuple-element.69), channel_id=1, replica_groups=mesh['tok'=8,'lat'=32] {'tok'}, dimensions={0}, use_global_device_ids=true | all-gather | bytes 1032192 | tf_op jit(solution)/shard_map/all_gather | solution.py:418
  36.5 13.5 %all_gather.19.loans_b = bf16[448,1024]{1,0:T(8,128)(2,1)S(1)} all-gather(bf16[56,1024]{1,0:T(8,128)(2,1)S(1)} %get-tuple-element.72), channel_id=1, replica_groups=mesh['tok'=8,'lat'=32] {'tok'}, dimensions={0}, use_global_device_ids=true | all-gather | bytes 1032192 | tf_op jit(solution)/shard_map/all_gather | solution.py:420
  50.0 7.4 %second_slots.1 = (bf16[512,2048]{1,0:T(8,128)(2,1)}, s32[8,128]{1,0:T(8,128)S(1)}, f32[8,128]{1,0:T(8,128)S(1)}) custom-call(s32[1]{0:T(128)} %bitcast.7.group, bf16[128,8192]{1,0:T(8,128)(2,1)} %tokens.3, bf16[448,1024]{1,0:T(8,128)(2,1)S(1)} %all_gather.18.loans_a, bf16[448,1024]{1,0:T(8,128)(2,1)S(1)} %all_gather.19.loans_b), custom_call_target="tpu_custom_call" | custom-call | flops 1073741824 | bytes 5242880 | tf_op jit(solution)/shard_map/second_slots/pallas_call | solution.py:422
  57.5 13.9 %all-to-all-done.2 = bf16[64,8,2048]{2,1,0:T(8,128)(2,1)} async-done(((bf16[64,8,2048]{2,1,0:T(8,128)(2,1)}), bf16[64,8,2048]{2,1,0:T(8,128)(2,1)}, u32[]{:S(2)}, u32[]{:S(2)}) %all-to-all-start.2) | async-done | bytes 2097184 | tf_op jit(solution)/shard_map/all_to_all | solution.py:408
  71.3 0.0 copy-start.4
  71.3 0.0 copy-start.9
  71.3 6.0 %all-to-all-start.1 = ((bf16[64,8,2048]{2,1,0:T(8,128)(2,1)}), bf16[64,8,2048]{2,1,0:T(8,128)(2,1)}, u32[]{:S(2)}, u32[]{:S(2)}) async-start(bf16[64,8,2048]{2,1,0:T(8,128)(2,1)} %bitcast.10), calls=%async_computation.1 | async-start | bytes 4194304 | tf_op jit(solution)/shard_map/all_to_all | solution.py:408
  77.4 12.1 %all-gather = f32[32,128]{1,0:T(8,128)S(1)} all-gather(f32[8,128]{1,0:T(8,128)S(1)} %get-tuple-element.77), channel_id=2, replica_groups={{0,1,2,3},{4,5,6,7},{8,9,10,11},{12,13,14,15},{16,17,18,19},{20,21,22,2..., dimensions={0}, use_global_device_ids=true | all-gather | bytes 20480 | tf_op jit(solution)/shard_map/all_gather | solution.py:440
  89.5 53.3 %all-gather.1 = f32[64,128]{1,0:T(8,128)S(1)} all-gather(f32[8,128]{1,0:T(8,128)S(1)} %bitcast_reduce_fusion.1), channel_id=3, replica_groups={{0,4,8,12,16,20,24,28},{1,5,9,13,17,21,25,29},{2,6,10,14,18,22,26,30},{..., dimensions={0}, use_global_device_ids=true | all-gather | bytes 36864 | tf_op jit(solution)/shard_map/all_gather | solution.py:440
  142.8 0.5 slice.24
  143.3 0.0 copy-done
  143.3 0.1 dynamic-slice_bitcast_fusion.bias
  143.4 0.1 pad_add_fusion.at
  143.5 0.0 copy-done.4
  143.5 0.0 copy-done.9
  143.5 10.3 %chunk_gradients.3.parts_in = f32[2,4,128,1024]{3,2,1,0:T(8,128)} custom-call(s32[2]{0:T(128)S(1)} %pad_add_fusion.at, bf16[512,2048]{1,0:T(8,128)(2,1)} %bitcast.15.chunk_in, bf16[128,8192]{1,0:T(8,128)(2,1)S(1)} %copy-done.4, bf16[128,8192]{1,0:T(8,128)(2,1)} %dec_in.3, f32[1,64]{1,0:T(1,128)S(1)} %dynamic-slice_bitcast_fusion.bias, f32[1,8192]{1,0:T(1,128)S(1)} %bitcast.36), custom_call_target="tpu_custom_call" | custom-call | flops 2684354560 | bytes 12582912 | tf_op jit(solution)/shard_map/chunk_gradients/pallas_call | solution.py:466
  153.8 0.0 all-to-all-done.1
  153.8 9.3 %last_gradients.1 = (f32[4,128,1024]{2,1,0:T(8,128)}, bf16[4,128,1024]{2,1,0:T(8,128)(2,1)S(1)}) custom-call(s32[2]{0:T(128)S(1)} %pad_add_fusion.at, bf16[512,2048]{1,0:T(8,128)(2,1)} %bitcast.11.chunk_in, bf16[128,8192]{1,0:T(8,128)(2,1)S(1)} %copy-done.4, bf16[128,8192]{1,0:T(8,128)(2,1)} %dec_in.3, f32[1,64]{1,0:T(1,128)S(1)} %dynamic-slice_bitcast_fusion.bias, ...), custom_call_target="tpu_custom_call" | custom-call | flops 2684354560 | bytes 12582912 | tf_op jit(solution)/shard_map/last_gradients/pallas_call | solution.py:467
  163.1 0.6 while.11
  163.8 0.1 collective-permute-start
  163.9 2.6 %collective-permute-done = bf16[4,128,1024]{2,1,0:T(8,128)(2,1)S(1)} collective-permute-done((bf16[4,128,1024]{2,1,0:T(8,128)(2,1)S(1)}, bf16[4,128,1024]{2,1,0:T(8,128)(2,1)S(1)}, u32[]{:S(2)}, u32[]{:S(2)}) %collective-permute-start) | collective-permute-done | bytes 1048608 | tf_op jit(solution)/shard_map/ppermute | solution.py:505
  166.5 1.9 %add_convert_fusion = bf16[4,128,1024]{2,1,0:T(8,128)(2,1)S(1)} fusion(f32[4,128,1024]{2,1,0:T(8,128)} %get-tuple-element.154, bf16[4,128,1024]{2,1,0:T(8,128)(2,1)S(1)} %collective-permute-done), kind=kLoop, calls=%fused_computation.74 | loop fusion | flops 1572864 | bytes 4194304 | tf_op jit(solution)/shard_map/convert_element_type | solution.py:506
  168.5 19.6 %all_to_all.19 = bf16[4,128,1024]{2,1,0:T(8,128)(2,1)S(1)} all-to-all(bf16[4,128,1024]{2,1,0:T(8,128)(2,1)S(1)} %add_convert_fusion), channel_id=1, replica_groups={{0,64,128,192},{32,96,160,224},{1,65,129,193},{33,97,161,225},{2,66,130..., dimensions={0} | all-to-all | bytes 2097152 | tf_op jit(solution)/shard_map/all_to_all | solution.py:507
  188.1 0.2 convert_reduce_fusion
  188.3 1.0 fusion.52
  (2 shorter events, 0.0 us)
Async XLA Ops:
  0.6 142.7 %copy-start = (f32[128]{0:T(128)S(1)}, f32[128]{0:T(128)}, u32[]{:S(2)}) copy-start(f32[128]{0:T(128)} %param.12) | copy-start | bytes 1540
  0.6 0.7 copy-start.1
  1.3 0.7 copy-start.2
  6.8 64.5 %all-to-all-start.2 = ((bf16[64,8,2048]{2,1,0:T(8,128)(2,1)}), bf16[64,8,2048]{2,1,0:T(8,128)(2,1)}, u32[]{:S(2)}, u32[]{:S(2)}) async-start(bf16[64,8,2048]{2,1,0:T(8,128)(2,1)} %bitcast.14), calls=%async_computation.2 | async-start | bytes 4194304 | tf_op jit(solution)/shard_map/all_to_all | solution.py:408
  71.3 72.2 %copy-start.4 = (bf16[128,8192]{1,0:T(8,128)(2,1)S(1)}, bf16[128,8192]{1,0:T(8,128)(2,1)}, u32[]{:S(2)}) copy-start(bf16[128,8192]{1,0:T(8,128)(2,1)} %enc_in.3) | copy-start | bytes 6291460
  71.3 72.2 %copy-start.9 = (f32[8192]{0:T(1024)S(1)}, f32[8192]{0:T(1024)}, u32[]{:S(2)}) copy-start(f32[8192]{0:T(1024)} %param.10) | copy-start | bytes 98308
  71.3 82.4 %all-to-all-start.1 = ((bf16[64,8,2048]{2,1,0:T(8,128)(2,1)}), bf16[64,8,2048]{2,1,0:T(8,128)(2,1)}, u32[]{:S(2)}, u32[]{:S(2)}) async-start(bf16[64,8,2048]{2,1,0:T(8,128)(2,1)} %bitcast.10), calls=%async_computation.1 | async-start | bytes 4194304 | tf_op jit(solution)/shard_map/all_to_all | solution.py:408
  163.8 2.7 %collective-permute-start = (bf16[4,128,1024]{2,1,0:T(8,128)(2,1)S(1)}, bf16[4,128,1024]{2,1,0:T(8,128)(2,1)S(1)}, u32[]{:S(2)}, u32[]{:S(2)}) collective-permute-start(bf16[4,128,1024]{2,1,0:T(8,128)(2,1)S(1)} %get-tuple-element.155), channel_id=1, source_target_pairs={{0,32},{32,0},{64,96},{96,64},{128,160},{160,128},{192,224},{224,1... | collective-permute-start | bytes 3145736 | tf_op jit(solution)/shard_map/ppermute | solution.py:505
where the time goes:
time: 190 us; the launch traced here: 189 us
  blocking collectives  115 us (61%)
  Pallas kernels  31.9 us (17%)
  starting transfers between devices  19.2 us (10%)
  waiting for transfers between devices  16.5 us (9%)
  local copies, waits for them, and re-layouts  2.98 us (2%)
  other arithmetic  2.25 us (1%)
    all_gather x2, blocking collectives, on_device(): flags = lax.all_gather(flags, 'lat', axis_index_groups=lines)  65.4 us
    all_to_all x1, blocking collectives, on_device(): lax.all_to_all(summed, 'tok', split_axis=0, concat_axis=0, tiled=True, ax...  19.6 us
    all_to_all x2, starting transfers between devices, exchange(): lax.all_to_all(shaped, ('tok', 'lat'), split_axis=0, concat_axis=0, tiled...  19.1 us
    all_gather x1, blocking collectives, on_device(): loans_a = lax.all_gather(lent_a, 'tok', tiled=True)  16.5 us
    all_to_all x2, waiting for transfers between devices, exchange(): lax.all_to_all(shaped, ('tok', 'lat'), split_axis=0, concat_axis=0, tiled...  13.9 us
    all_gather x1, blocking collectives, on_device(): loans_b = lax.all_gather(lent_b, 'tok', tiled=True)  13.5 us
    pallas_call x1, Pallas kernels, on_device(): part_call(scalars, got1, enc_weight, dec_weight, bias_row, offset_row)  10.3 us
    pallas_call x1, Pallas kernels, on_device(): pl.pallas_call(last_kernel, out_shape=[jax.ShapeDtypeStruct(half_shape, F...  9.32 us
  transfers between devices with their start and end apart: 3, of which 2 were waited for; matrix products, arithmetic and copies ran while one was open for 0% of the time, Pallas kernels for 9%

commit v1 on v0

--- a/solution.py
+++ b/solution.py
@@ -17,6 +17,7 @@
 GROUP = CUTS * SLOTS
 STRIDE = 8
 EMPTY = 2.0**100
+EXTRA = 128
 STEP = 1024
 PIECES = 8
 LENT = (6, 7)
@@ -68,25 +69,51 @@
     return [ref[:, h * part + i * STEP : h * part + (i + 1) * STEP] for h in range(CUTS)]
 
 
-def first_kernel(targets, ids, home, tokens, chunk, lent_a, lent_b):
+def places_of(ids, home):
+    total = home.shape[1]
+    named = flat(iota((total, ids.shape[1]), 0) == ids[...]).astype(BF)
+    table = jnp.broadcast_to(home[...], (8, total)).astype(F32).astype(BF)
+    return mm(table, named)[:1].astype(I32)
+
+
+def first_kernel(targets, ids, home, tokens_in, chunk_out, tokens, chunk, sems_in, sems_out):
     rows, width = tokens.shape
     part = width // CUTS
-    total = home.shape[1]
-    named = flat(iota((total, rows), 0) == ids[...]).astype(BF)
-    table = jnp.broadcast_to(home[...], (8, total)).astype(F32).astype(BF)
-    places = mm(table, named)[:1].astype(I32)
-    target = target_of(places, targets)
+    steps = part // STEP
+    loads = []
+    for i in range(steps):
+        for h in range(CUTS):
+            columns = pl.ds(h * part + i * STEP, STEP)
+            sem = sems_in.at[len(loads)]
+            loads.append(pltpu.make_async_copy(tokens_in.at[:, columns], tokens.at[:, columns], sem))
+            loads[-1].start()
+    target = target_of(places_of(ids, home), targets)
     unused, rank = ranks_of(target, targets)
-    rank = rank.astype(I32)
     codes, cut = slot_codes(targets, 0)
-    hit = flat(codes == target * STRIDE + rank)
+    hit = flat(codes == target * STRIDE + rank.astype(I32))
     wide = jnp.concatenate([jnp.where(cut == h, hit, 0.0) for h in range(CUTS)], axis=1)
     wide = wide.astype(BF)
     filled = jnp.sum(hit, axis=1, keepdims=True) > 0.5
-    for i in range(part // STEP):
+    stores = []
+    for i in range(steps):
+        for h in range(CUTS):
+            loads[i * CUTS + h].wait()
         got = mm(wide, jnp.concatenate(cut_columns(tokens, i), axis=0))
         chunk[:, i * STEP : (i + 1) * STEP] = jnp.where(filled, got, EMPTY).astype(BF)
-    over = flat(rank >= DIRECT)
+        columns = pl.ds(i * STEP, STEP)
+        stores.append(
+            pltpu.make_async_copy(chunk.at[:, columns], chunk_out.at[:, columns], sems_out.at[i])
+        )
+        stores[-1].start()
+    for store in stores:
+        store.wait()
+
+
+def lend_kernel(targets, ids, home, tokens, lent_a, lent_b):
+    rows = tokens.shape[0]
+    places = places_of(ids, home)
+    unused, rank = ranks_of(target_of(places, targets), targets)
+    over = flat(rank.astype(I32) >= DIRECT)
     order = mm(jnp.broadcast_to(over, (8, rows)).astype(BF), before(rows))[:1].astype(I32)
     first = 0
     for count, lent in zip(LENT, (lent_a, lent_b)):
@@ -106,7 +133,7 @@
         first += count
 
 
-def second_kernel(targets, group, tokens, loans_a, loans_b, chunk, left, flags):
+def second_kernel(targets, group, tokens, loans_a, loans_b, chunk, left):
     rows, width = tokens.shape
     part = width // CUTS
     lines = (LENT[0] + 1) * PIECES
@@ -173,7 +200,7 @@
     hit_b = flat(codes == codes_of_lines(LENT[0], LENT[1]))
     filled = jnp.sum(hit, axis=1, keepdims=True) + jnp.sum(hit_a, axis=1, keepdims=True)
     filled = filled + jnp.sum(hit_b, axis=1, keepdims=True) > 0.5
-    flags[...] = jnp.broadcast_to(flag, flags.shape)
+    chunk[:, part:] = jnp.broadcast_to(flag, (hit.shape[0], EXTRA)).astype(BF)
     per_cut = part // STEP
     piece = iota((1, size), 1) % PIECES
     for i in range(per_cut):
@@ -304,6 +331,7 @@
     parts_in,
     mine_out,
     other_out,
+    flags,
     chunk,
     enc,
     dec,
@@ -314,12 +342,14 @@
     parts,
     mine,
     other,
+    marks,
     sems_out,
 ):
     latents = enc.shape[0]
     core = at[0]
     ready = Loader(sems, at[1], chunk_in, enc_in, dec_in, chunk, enc, dec)
     ready.move("third", parts_in, parts)
+    ready.move("marks", chunk_in.at[:, pl.ds(chunk.shape[1], EXTRA)], marks)
 
     def out_copy(which, grad):
         source, result = ((mine, mine_out), (other, other_out))[which]
@@ -346,6 +376,8 @@
             out_copy(1, grad).start()
 
     gradient_body(chunk, enc, dec, bias, dec_bias, cent, err, acc, store, ready)
+    ready("marks", 0)
+    flags[0] = jnp.max(marks[...].astype(F32))
     for which in range(2):
         for grad in range(2):
             out_copy(which, grad).wait()
@@ -393,18 +425,35 @@
         flops=2 * slot_rows * CUTS * rows * part, bytes_accessed=5 * 2**20, transcendentals=0
     )
 
-    chunk1, lent_a, lent_b = pl.pallas_call(
+    ids_row = block_ids.reshape(1, rows)
+    home_row = block_home.reshape(1, -1)
+    chunk1 = pl.pallas_call(
         functools.partial(first_kernel, targets),
-        out_shape=[chunk_shape, lent_shape, lent_shape],
+        out_shape=chunk_shape,
+        in_specs=[vmem()] * 2 + [anywhere()],
+        out_specs=anywhere(),
+        scratch_shapes=[
+            pltpu.VMEM((rows, width), BF),
+            pltpu.VMEM((slot_rows, part), BF),
+            pltpu.SemaphoreType.DMA((CUTS * per_cut,)),
+            pltpu.SemaphoreType.DMA((per_cut,)),
+        ],
+        compiler_params=room(56),
+        cost_estimate=move_cost,
+        name="first_slots",
+    )(ids_row, home_row, tokens)
+    lent_a, lent_b = pl.pallas_call(
+        functools.partial(lend_kernel, targets),
+        out_shape=[lent_shape, lent_shape],
         in_specs=[vmem()] * 3,
-        out_specs=[vmem()] * 3,
+        out_specs=[vmem()] * 2,
         compiler_params=room(20),
         cost_estimate=move_cost,
-        name="first_slots",
-    )(block_ids.reshape(1, rows), block_home.reshape(1, -1), tokens)
+        name="lent_rows",
+    )(ids_row, home_row, tokens)
 
     def exchange(chunk):
-        shaped = chunk.reshape(targets, GROUP, part)
+        shaped = chunk.reshape(targets, GROUP, chunk.shape[1])
         got = lax.all_to_all(
             shaped,
             ("tok", "lat"),
@@ -413,33 +462,25 @@
             tiled=True,
             axis_index_groups=exchange_groups,
         )
-        return got.reshape(slot_rows, part)
+        return got.reshape(chunk.shape)
 
     loans_a = lax.all_gather(lent_a, "tok", tiled=True)
     loans_a, lent_b = lax.optimization_barrier((loans_a, lent_b))
     loans_b = lax.all_gather(lent_b, "tok", tiled=True)
     got1 = exchange(chunk1)
-    chunk2, left, flags = pl.pallas_call(
+    chunk2, left = pl.pallas_call(
         functools.partial(second_kernel, targets),
         out_shape=[
-            chunk_shape,
+            jax.ShapeDtypeStruct((slot_rows, part + EXTRA), BF),
             jax.ShapeDtypeStruct((8, rows), I32),
-            jax.ShapeDtypeStruct((8, rows), F32),
         ],
         in_specs=[smem()] + [vmem()] * 3,
-        out_specs=[vmem()] * 3,
+        out_specs=[vmem()] * 2,
         compiler_params=room(24),
         cost_estimate=move_cost,
         name="second_slots",
     )(me.reshape(1), tokens, loans_a, loans_b)
     got2 = exchange(chunk2)
-    line = 4
-    along_x = [[i * line + j for j in range(line)] for i in range(lat_count // line)]
-    along_z = [[i * line + j for i in range(lat_count // line)] for j in range(line)]
-    for lines in (along_x, along_z):
-        flags = lax.all_gather(flags, "lat", axis_index_groups=lines)
-        flags = jnp.max(flags, axis=0)
-
     bias_row = lax.dynamic_slice_in_dim(enc_bias, first_row, latents).reshape(1, latents)
     offset_row = dec_bias.reshape(1, width)
     work = [
@@ -449,7 +490,7 @@
         pltpu.VMEM((slot_rows, part), BF),
         pltpu.VMEM((slot_rows, part), BF),
         pltpu.VMEM((slot_rows, CUTS * latents), F32),
-        pltpu.SemaphoreType.DMA((per_cut * (CUTS + 1) + 2,)),
+        pltpu.SemaphoreType.DMA((per_cut * (CUTS + 1) + 3,)),
     ]
     parts_shape = (per_cut, CUTS, 2 * latents, STEP)
     half_shape = (CUTS, 2 * latents, STEP)
@@ -464,19 +505,21 @@
         name="chunk_gradients",
     )
     parts = part_call(scalars, got1, enc_weight, dec_weight, bias_row, offset_row)
-    mine, other = pl.pallas_call(
+    mine, other, flags = pl.pallas_call(
         last_kernel,
         out_shape=[
             jax.ShapeDtypeStruct(half_shape, F32),
             jax.ShapeDtypeStruct(half_shape, BF),
+            jax.ShapeDtypeStruct((1,), F32),
         ],
         in_specs=[smem()] + [anywhere()] * 3 + [vmem()] * 2 + [anywhere()],
-        out_specs=[anywhere()] * 2,
+        out_specs=[anywhere()] * 2 + [smem()],
         scratch_shapes=[
             *work,
             pltpu.VMEM(parts_shape, F32),
             pltpu.VMEM(half_shape, F32),
             pltpu.VMEM(half_shape, BF),
+            pltpu.VMEM((slot_rows, EXTRA), BF),
             pltpu.SemaphoreType.DMA((4,)),
         ],
         compiler_params=room(56),
@@ -500,7 +543,7 @@
         return mine, (other.astype(F32) + more).astype(BF), jnp.zeros((), F32)
 
     mine, other, unused = lax.while_loop(
-        lambda carry: carry[2] > 0.5, rest, (mine, other, flags[0, 0])
+        lambda carry: carry[2] > 0.5, rest, (mine, other, flags.reshape(()))
     )
     swapped = lax.ppermute(other, "tok", [(i, i ^ 1) for i in range(groups)])
     summed = (mine + swapped.astype(F32)).astype(BF)

time: 190 us -> 166 us (0.87)
  blocking collectives: 115 us -> 48.1 us
  waiting for transfers between devices: 16.5 us -> 61.3 us
    all_gather x2 -> x0, blocking collectives: 65.4 us -> none  [on_device(): flags = lax.all_gather(flags, 'lat', axis_index_groups=lines)]
    all_to_all x2, waiting for transfers between devices: 13.9 us -> 58.6 us  [exchange(): lax.all_to_all(shaped, ('tok', 'lat'), split_axis=0, concat_axis=0, tiled...]
    pallas_call x2 -> x3, Pallas kernels: 12.3 us -> 11.4 us  [the longest x1 5.96 us: on_device(): pl.pallas_call(functools.partial(second_kernel, targets), out_shape=[jax....]
  transfers between devices with their start and end apart: 3 -> 3, of which waited for: 2 -> 3; matrix products, arithmetic and copies ran while one was open for 0% -> 0% of each run, Pallas kernels for 9% -> 10%
where the time goes in v1:
time: 166 us; the launch traced here: 165 us
  waiting for transfers between devices  61.3 us (37%)
  blocking collectives  48.1 us (29%)
  Pallas kernels  31.7 us (19%)
  starting transfers between devices  19.4 us (12%)
  other arithmetic  2.23 us (1%)
    all_to_all x2, waiting for transfers between devices, exchange(): lax.all_to_all(shaped, ('tok', 'lat'), split_axis=0, concat_axis=0, tiled...  58.6 us
    all_to_all x1, blocking collectives, on_device(): lax.all_to_all(summed, 'tok', split_axis=0, concat_axis=0, tiled=True, ax...  19.4 us
    all_to_all x2, starting transfers between devices, exchange(): lax.all_to_all(shaped, ('tok', 'lat'), split_axis=0, concat_axis=0, tiled...  19.3 us
    all_gather x1, blocking collectives, on_device(): loans_a = lax.all_gather(lent_a, 'tok', tiled=True)  15.3 us
    all_gather x1, blocking collectives, on_device(): loans_b = lax.all_gather(lent_b, 'tok', tiled=True)  13.5 us
    pallas_call x1, Pallas kernels, on_device(): part_call(scalars, got1, enc_weight, dec_weight, bias_row, offset_row)  10.3 us
    pallas_call x1, Pallas kernels, on_device(): pl.pallas_call(last_kernel, out_shape=[jax.ShapeDtypeStruct(half_shape, F...  10 us
    pallas_call x1, Pallas kernels, on_device(): pl.pallas_call(functools.partial(second_kernel, targets), out_shape=[jax....  5.96 us
  transfers between devices with their start and end apart: 3, of which 3 were waited for; matrix products, arithmetic and copies ran while one was open for 0% of the time, Pallas kernels for 10%

profile of v1, /device:TPU:6, one launch (start us, length us, event | category | flops | bytes accessed | tf_op | source)
XLA Modules:
  0.0 165.4 jit_solution(12238200072919294254)
XLA Ops:
  0.6 0.0 copy-start
  0.6 4.4 %first_slots.1 = bf16[512,2048]{1,0:T(8,128)(2,1)} custom-call(s32[1,128]{1,0:T(1,128)} %bitcast.28, s32[1,64]{1,0:T(1,128)} %bitcast.30, bf16[128,8192]{1,0:T(8,128)(2,1)} %tokens_in.1), custom_call_target="tpu_custom_call" | custom-call | flops 1073741824 | bytes 5242880 | tf_op jit(solution)/shard_map/first_slots/pallas_call | solution.py:430
  5.0 0.0 copy-start.1
  5.0 0.0 copy-start.2
  5.1 0.0 copy-start.6
  5.1 13.3 %all-to-all-start.2 = ((bf16[64,8,2048]{2,1,0:T(8,128)(2,1)}), bf16[64,8,2048]{2,1,0:T(8,128)(2,1)}, u32[]{:S(2)}, u32[]{:S(2)}) async-start(bf16[64,8,2048]{2,1,0:T(8,128)(2,1)} %bitcast.33), calls=%async_computation.2 | async-start | bytes 4194304 | tf_op jit(solution)/shard_map/all_to_all | solution.py:457
  18.4 0.0 copy-done.1
  18.4 0.0 copy-done.2
  18.4 0.0 copy-done.6
  18.4 1.1 lent_rows.1
  19.5 15.3 %all_gather.6.loans_a = bf16[448,1024]{1,0:T(8,128)(2,1)S(1)} all-gather(bf16[56,1024]{1,0:T(8,128)(2,1)S(1)} %get-tuple-element.68), channel_id=1, replica_groups=mesh['tok'=8,'lat'=32] {'tok'}, dimensions={0}, use_global_device_ids=true | all-gather | bytes 1032192 | tf_op jit(solution)/shard_map/all_gather | solution.py:467
  34.8 13.5 %all_gather.7.loans_b = bf16[448,1024]{1,0:T(8,128)(2,1)S(1)} all-gather(bf16[56,1024]{1,0:T(8,128)(2,1)S(1)} %get-tuple-element.71), channel_id=1, replica_groups=mesh['tok'=8,'lat'=32] {'tok'}, dimensions={0}, use_global_device_ids=true | all-gather | bytes 1032192 | tf_op jit(solution)/shard_map/all_gather | solution.py:469
  48.3 6.0 %second_slots.1 = (bf16[512,2176]{1,0:T(8,128)(2,1)}, s32[8,128]{1,0:T(8,128)S(1)}) custom-call(s32[1]{0:T(128)} %bitcast.7.group, bf16[128,8192]{1,0:T(8,128)(2,1)S(1)} %copy-done.6, bf16[448,1024]{1,0:T(8,128)(2,1)S(1)} %all_gather.6.loans_a, bf16[448,1024]{1,0:T(8,128)(2,1)S(1)} %all_gather.7.loans_b), custom_call_target="tpu_custom_call" | custom-call | flops 1073741824 | bytes 5242880 | tf_op jit(solution)/shard_map/second_slots/pallas_call | solution.py:471
  54.2 15.4 %all-to-all-done.2 = bf16[64,8,2048]{2,1,0:T(8,128)(2,1)} async-done(((bf16[64,8,2048]{2,1,0:T(8,128)(2,1)}), bf16[64,8,2048]{2,1,0:T(8,128)(2,1)}, u32[]{:S(2)}, u32[]{:S(2)}) %all-to-all-start.2) | async-done | bytes 2097184 | tf_op jit(solution)/shard_map/all_to_all | solution.py:457
  69.7 0.0 copy-start.4
  69.7 0.0 copy-start.10
  69.7 6.0 %all-to-all-start.1 = ((bf16[64,8,2176]{2,1,0:T(8,128)(2,1)}), bf16[64,8,2176]{2,1,0:T(8,128)(2,1)}, u32[]{:S(2)}, u32[]{:S(2)}) async-start(bf16[64,8,2176]{2,1,0:T(8,128)(2,1)} %bitcast.10), calls=%async_computation.1 | async-start | bytes 4456448 | tf_op jit(solution)/shard_map/all_to_all | solution.py:457
  75.7 0.0 copy-done
  75.7 0.1 dynamic-slice_bitcast_fusion.bias
  75.8 0.1 pad_add_fusion.at
  75.9 0.0 copy-done.4
  75.9 0.0 copy-done.10
  75.9 10.3 %chunk_gradients.3.parts_in = f32[2,4,128,1024]{3,2,1,0:T(8,128)} custom-call(s32[2]{0:T(128)S(1)} %pad_add_fusion.at, bf16[512,2048]{1,0:T(8,128)(2,1)} %bitcast.15.chunk_in, bf16[128,8192]{1,0:T(8,128)(2,1)S(1)} %copy-done.4, bf16[128,8192]{1,0:T(8,128)(2,1)} %dec_in.3, f32[1,64]{1,0:T(1,128)S(1)} %dynamic-slice_bitcast_fusion.bias, f32[1,8192]{1,0:T(1,128)S(1)} %bitcast.35), custom_call_target="tpu_custom_call" | custom-call | flops 2684354560 | bytes 12582912 | tf_op jit(solution)/shard_map/chunk_gradients/pallas_call | solution.py:507
  86.2 43.2 %all-to-all-done.1 = bf16[64,8,2176]{2,1,0:T(8,128)(2,1)} async-done(((bf16[64,8,2176]{2,1,0:T(8,128)(2,1)}), bf16[64,8,2176]{2,1,0:T(8,128)(2,1)}, u32[]{:S(2)}, u32[]{:S(2)}) %all-to-all-start.1) | async-done | bytes 2228256 | tf_op jit(solution)/shard_map/all_to_all | solution.py:457
  129.4 10.0 %last_gradients.1 = (f32[4,128,1024]{2,1,0:T(8,128)}, bf16[4,128,1024]{2,1,0:T(8,128)(2,1)S(1)}, f32[1]{0:T(128)}) custom-call(s32[2]{0:T(128)S(1)} %pad_add_fusion.at, bf16[512,2176]{1,0:T(8,128)(2,1)} %bitcast.11.chunk_in, bf16[128,8192]{1,0:T(8,128)(2,1)S(1)} %copy-done.4, bf16[128,8192]{1,0:T(8,128)(2,1)} %dec_in.3, ...), custom_call_target="tpu_custom_call" | custom-call | flops 2684354560 | bytes 12582912 | tf_op jit(solution)/shard_map/last_gradients/pallas_call | solution.py:508
  139.4 0.7 while.11
  140.1 0.1 collective-permute-start
  140.2 2.6 %collective-permute-done = bf16[4,128,1024]{2,1,0:T(8,128)(2,1)S(1)} collective-permute-done((bf16[4,128,1024]{2,1,0:T(8,128)(2,1)S(1)}, bf16[4,128,1024]{2,1,0:T(8,128)(2,1)S(1)}, u32[]{:S(2)}, u32[]{:S(2)}) %collective-permute-start) | collective-permute-done | bytes 1048608 | tf_op jit(solution)/shard_map/ppermute | solution.py:548
  142.8 1.9 %add_convert_fusion = bf16[4,128,1024]{2,1,0:T(8,128)(2,1)S(1)} fusion(f32[4,128,1024]{2,1,0:T(8,128)} %get-tuple-element.152, bf16[4,128,1024]{2,1,0:T(8,128)(2,1)S(1)} %collective-permute-done), kind=kLoop, calls=%fused_computation.74 | loop fusion | flops 1572864 | bytes 4194304 | tf_op jit(solution)/shard_map/convert_element_type | solution.py:549
  144.8 19.4 %all_to_all.19 = bf16[4,128,1024]{2,1,0:T(8,128)(2,1)S(1)} all-to-all(bf16[4,128,1024]{2,1,0:T(8,128)(2,1)S(1)} %add_convert_fusion), channel_id=1, replica_groups={{0,64,128,192},{32,96,160,224},{1,65,129,193},{33,97,161,225},{2,66,130..., dimensions={0} | all-to-all | bytes 2097152 | tf_op jit(solution)/shard_map/all_to_all | solution.py:550
  164.1 0.2 convert_reduce_fusion
  164.4 1.0 fusion.52
Async XLA Ops:
  0.6 75.1 %copy-start = (f32[128]{0:T(128)S(1)}, f32[128]{0:T(128)}, u32[]{:S(2)}) copy-start(f32[128]{0:T(128)} %param.12) | copy-start | bytes 1540
  5.0 13.4 %copy-start.1 = (s32[128,1]{0,1:T(1,128)S(1)}, s32[128,1]{0,1:T(1,128)}, u32[]{:S(2)}) copy-start(s32[128,1]{0,1:T(1,128)} %param.14) | copy-start | bytes 1540
  5.0 13.4 %copy-start.2 = (s32[64]{0:T(128)S(1)}, s32[64]{0:T(128)}, u32[]{:S(2)}) copy-start(s32[64]{0:T(128)} %param.15) | copy-start | bytes 772
  5.1 13.4 %copy-start.6 = (bf16[128,8192]{1,0:T(8,128)(2,1)S(1)}, bf16[128,8192]{1,0:T(8,128)(2,1)}, u32[]{:S(2)}) copy-start(bf16[128,8192]{1,0:T(8,128)(2,1)} %tokens_in.1) | copy-start | bytes 6291460
  5.1 64.6 %all-to-all-start.2 = ((bf16[64,8,2048]{2,1,0:T(8,128)(2,1)}), bf16[64,8,2048]{2,1,0:T(8,128)(2,1)}, u32[]{:S(2)}, u32[]{:S(2)}) async-start(bf16[64,8,2048]{2,1,0:T(8,128)(2,1)} %bitcast.33), calls=%async_computation.2 | async-start | bytes 4194304 | tf_op jit(solution)/shard_map/all_to_all | solution.py:457
  69.7 6.2 %copy-start.4 = (bf16[128,8192]{1,0:T(8,128)(2,1)S(1)}, bf16[128,8192]{1,0:T(8,128)(2,1)}, u32[]{:S(2)}) copy-start(bf16[128,8192]{1,0:T(8,128)(2,1)} %enc_in.3) | copy-start | bytes 6291460
  69.7 6.2 %copy-start.10 = (f32[8192]{0:T(1024)S(1)}, f32[8192]{0:T(1024)}, u32[]{:S(2)}) copy-start(f32[8192]{0:T(1024)} %param.10) | copy-start | bytes 98308
  69.7 59.7 %all-to-all-start.1 = ((bf16[64,8,2176]{2,1,0:T(8,128)(2,1)}), bf16[64,8,2176]{2,1,0:T(8,128)(2,1)}, u32[]{:S(2)}, u32[]{:S(2)}) async-start(bf16[64,8,2176]{2,1,0:T(8,128)(2,1)} %bitcast.10), calls=%async_computation.1 | async-start | bytes 4456448 | tf_op jit(solution)/shard_map/all_to_all | solution.py:457
  140.1 2.7 %collective-permute-start = (bf16[4,128,1024]{2,1,0:T(8,128)(2,1)S(1)}, bf16[4,128,1024]{2,1,0:T(8,128)(2,1)S(1)}, u32[]{:S(2)}, u32[]{:S(2)}) collective-permute-start(bf16[4,128,1024]{2,1,0:T(8,128)(2,1)S(1)} %get-tuple-element.153), channel_id=1, source_target_pairs={{0,32},{32,0},{64,96},{96,64},{128,160},{160,128},{192,224},{224,1... | collective-permute-start | bytes 3145736 | tf_op jit(solution)/shard_map/ppermute | solution.py:548

commit v2 on v1

--- a/solution.py
+++ b/solution.py
@@ -215,7 +215,7 @@
     rows, part = chunk.shape
     latents = enc.shape[0]
     steps = part // STEP
-    inner = iota((rows, 1), 0) % GROUP
+    inner = iota((1, rows), 1) % GROUP
     cut = inner // SLOTS
     cut8 = iota((GROUP, 1), 0) // SLOTS
 
@@ -229,19 +229,19 @@
         return value[None]
 
     def joined(total):
-        own = total[:, :latents]
+        own = total[:latents]
         for h in range(1, CUTS):
-            own = jnp.where(cut == h, total[:, h * latents : (h + 1) * latents], own)
+            own = jnp.where(cut == h, total[h * latents : (h + 1) * latents], own)
         shift = GROUP // 2
         while shift >= SLOTS:
-            down = pltpu.roll(own, rows - shift, 0)
-            wrapped = pltpu.roll(own, GROUP - shift, 0)
+            down = pltpu.roll(own, rows - shift, 1)
+            wrapped = pltpu.roll(own, GROUP - shift, 1)
             own = own + jnp.where(inner < GROUP - shift, down, wrapped)
             shift //= 2
         return own
 
     def spread(values):
-        return jnp.concatenate([jnp.where(cut == h, values, 0.0) for h in range(CUTS)], axis=1)
+        return jnp.concatenate([jnp.where(cut == h, values, 0.0) for h in range(CUTS)], axis=0)
 
     for i in range(steps):
         ready("first", i)
@@ -250,14 +250,16 @@
         cent[:, here(i)] = c
         w = jnp.concatenate(cut_columns(enc, i), axis=0)
         if i == 0:
-            acc[...] = mm_t(c, w)
+            acc[...] = mm_t(w, c)
         else:
-            acc[...] += mm_t(c, w)
-    valid = chunk[:, :latents].astype(F32) < EMPTY / 2
+            acc[...] += mm_t(w, c)
+    filled = flat(chunk[:, :128].astype(F32) < EMPTY / 2).astype(BF)
+    valid = mm_t(flat(iota((8, 128), 1) == 0).astype(BF), filled)[:1] > 0.5
     pre = joined(acc[...]) + bias[...]
     gate = 1.0 / (1.0 + jnp.exp(-pre))
     latent = spread(jnp.where(valid, pre * gate, 0.0))
-    latent_b = latent.astype(BF)
+    latent_t = latent.astype(BF)
+    latent_b = latent.T.astype(BF)
     ready("second", 0)
     for i in range(steps):
         w = jnp.concatenate(cut_columns(dec, i), axis=0)
@@ -266,13 +268,12 @@
         e = ((offset(i) + d - x) * (1.0 / 32.0)).reshape(rows, STEP).astype(BF)
         err[:, here(i)] = e
         if i == 0:
-            acc[...] = mm_t(e, w)
+            acc[...] = mm_t(w, e)
         else:
-            acc[...] += mm_t(e, w)
+            acc[...] += mm_t(w, e)
     dlatent = joined(acc[...])
     dpre = spread(jnp.where(valid, dlatent * gate * (1.0 + pre * (1.0 - gate)), 0.0))
-    dpre_t = dpre.T.astype(BF)
-    latent_t = latent.T.astype(BF)
+    dpre_t = dpre.astype(BF)
     ready("third", 0)
     for i in range(steps):
         store(i, 0, mm(dpre_t, cent[:, here(i)]))
@@ -307,49 +308,19 @@
             self.moves[stage].wait()
 
 
-def part_kernel(
-    at, chunk_in, enc_in, dec_in, bias, dec_bias, parts, chunk, enc, dec, cent, err, acc, sems
-):
-    latents = enc.shape[0]
-    ready = Loader(sems, at[1], chunk_in, enc_in, dec_in, chunk, enc, dec)
-
-    def store(i, grad, value):
-        rows = slice(grad * latents, (grad + 1) * latents)
-        for h in range(CUTS):
-            parts[i, h, rows] = value[h * latents : (h + 1) * latents]
-
-    gradient_body(chunk, enc, dec, bias, dec_bias, cent, err, acc, store, ready)
-
-
-def last_kernel(
-    at,
-    chunk_in,
-    enc_in,
-    dec_in,
-    bias,
-    dec_bias,
-    parts_in,
-    mine_out,
-    other_out,
-    flags,
-    chunk,
-    enc,
-    dec,
-    cent,
-    err,
-    acc,
-    sems,
-    parts,
-    mine,
-    other,
-    marks,
-    sems_out,
-):
+def chunk_kernel(with_prior, at, chunk_in, enc_in, dec_in, bias, dec_bias, *refs):
+    refs = list(refs)
+    prior_in = refs.pop(0) if with_prior else None
+    mine_out, other_out = refs.pop(0), refs.pop(0)
+    flags = refs.pop(0) if with_prior else None
+    chunk, enc, dec, cent, err, acc, sems, mine, other, sems_out = refs[:10]
     latents = enc.shape[0]
     core = at[0]
     ready = Loader(sems, at[1], chunk_in, enc_in, dec_in, chunk, enc, dec)
-    ready.move("third", parts_in, parts)
-    ready.move("marks", chunk_in.at[:, pl.ds(chunk.shape[1], EXTRA)], marks)
+    if with_prior:
+        prior, marks = refs[10:]
+        ready.move("third", prior_in, prior)
+        ready.move("marks", chunk_in.at[:, pl.ds(chunk.shape[1], EXTRA)], marks)
 
     def out_copy(which, grad):
         source, result = ((mine, mine_out), (other, other_out))[which]
@@ -359,25 +330,24 @@
 
     def store(i, grad, value):
         rows = slice(grad * latents, (grad + 1) * latents)
-        totals = [
-            value[h * latents : (h + 1) * latents] + parts[i, h, rows] for h in range(CUTS)
-        ]
+        cuts = [value[h * latents : (h + 1) * latents] for h in range(CUTS)]
 
         @pl.when(core == i)
         def _():
             for h in range(CUTS):
-                mine[h, rows] = totals[h]
+                mine[h, rows] = cuts[h] + prior[h, rows] if with_prior else cuts[h]
             out_copy(0, grad).start()
 
         @pl.when(core != i)
         def _():
             for h in range(CUTS):
-                other[h, rows] = totals[h].astype(BF)
+                other[h, rows] = cuts[h].astype(other.dtype)
             out_copy(1, grad).start()
 
     gradient_body(chunk, enc, dec, bias, dec_bias, cent, err, acc, store, ready)
-    ready("marks", 0)
-    flags[0] = jnp.max(marks[...].astype(F32))
+    if with_prior:
+        ready("marks", 0)
+        flags[0] = jnp.max(marks[...].astype(F32))
     for which in range(2):
         for grad in range(2):
             out_copy(which, grad).wait()
@@ -389,6 +359,10 @@
 
 def anywhere():
     return pl.BlockSpec(memory_space=pl.ANY)
+
+
+def hbm():
+    return pl.BlockSpec(memory_space=pltpu.HBM)
 
 
 def smem():
@@ -481,51 +455,58 @@
         name="second_slots",
     )(me.reshape(1), tokens, loans_a, loans_b)
     got2 = exchange(chunk2)
-    bias_row = lax.dynamic_slice_in_dim(enc_bias, first_row, latents).reshape(1, latents)
+    bias_row = lax.dynamic_slice_in_dim(enc_bias, first_row, latents).reshape(latents, 1)
     offset_row = dec_bias.reshape(1, width)
-    work = [
-        pltpu.VMEM((slot_rows, part), BF),
-        pltpu.VMEM((latents, width), BF),
-        pltpu.VMEM((latents, width), BF),
-        pltpu.VMEM((slot_rows, part), BF),
-        pltpu.VMEM((slot_rows, part), BF),
-        pltpu.VMEM((slot_rows, CUTS * latents), F32),
-        pltpu.SemaphoreType.DMA((per_cut * (CUTS + 1) + 3,)),
-    ]
-    parts_shape = (per_cut, CUTS, 2 * latents, STEP)
     half_shape = (CUTS, 2 * latents, STEP)
+
+    def work(kind):
+        return [
+            pltpu.VMEM((slot_rows, part), BF),
+            pltpu.VMEM((latents, width), BF),
+            pltpu.VMEM((latents, width), BF),
+            pltpu.VMEM((slot_rows, part), BF),
+            pltpu.VMEM((slot_rows, part), BF),
+            pltpu.VMEM((CUTS * latents, slot_rows), F32),
+            pltpu.SemaphoreType.DMA((per_cut * (CUTS + 1) + 3,)),
+            pltpu.VMEM(half_shape, F32),
+            pltpu.VMEM(half_shape, kind),
+            pltpu.SemaphoreType.DMA((4,)),
+        ]
+
+    def swap(values):
+        return lax.ppermute(values, "tok", [(i, i ^ 1) for i in range(groups)])
+
+    operands = (enc_weight, dec_weight, bias_row, offset_row)
     part_call = pl.pallas_call(
-        part_kernel,
-        out_shape=jax.ShapeDtypeStruct(parts_shape, F32),
-        in_specs=[smem()] + [anywhere()] * 3 + [vmem()] * 2,
-        out_specs=vmem(),
-        scratch_shapes=work,
+        functools.partial(chunk_kernel, False),
+        out_shape=[jax.ShapeDtypeStruct(half_shape, F32)] * 2,
+        in_specs=[smem()] + [hbm()] * 3 + [vmem()] * 2,
+        out_specs=[hbm()] * 2,
+        scratch_shapes=work(F32),
         compiler_params=room(56),
         cost_estimate=matmul_cost,
         name="chunk_gradients",
     )
-    parts = part_call(scalars, got1, enc_weight, dec_weight, bias_row, offset_row)
+    mine1, other1 = part_call(scalars, got1, *operands)
+    prior = mine1 + swap(other1)
     mine, other, flags = pl.pallas_call(
-        last_kernel,
+        functools.partial(chunk_kernel, True),
         out_shape=[
             jax.ShapeDtypeStruct(half_shape, F32),
             jax.ShapeDtypeStruct(half_shape, BF),
             jax.ShapeDtypeStruct((1,), F32),
         ],
-        in_specs=[smem()] + [anywhere()] * 3 + [vmem()] * 2 + [anywhere()],
+        in_specs=[smem(), anywhere()] + [hbm()] * 2 + [vmem()] * 2 + [hbm()],
         out_specs=[anywhere()] * 2 + [smem()],
         scratch_shapes=[
-            *work,
-            pltpu.VMEM(parts_shape, F32),
+            *work(BF),
             pltpu.VMEM(half_shape, F32),
-            pltpu.VMEM(half_shape, BF),
             pltpu.VMEM((slot_rows, EXTRA), BF),
-            pltpu.SemaphoreType.DMA((4,)),
         ],
         compiler_params=room(56),
         cost_estimate=matmul_cost,
         name="last_gradients",
-    )(scalars, got2, enc_weight, dec_weight, bias_row, offset_row, parts)
+    )(scalars, got2, *operands, prior)
 
     def rest(carry):
         mine, other, unused = carry
@@ -537,16 +518,13 @@
             data = data + mm(chosen, tokens[:, h * part : (h + 1) * part])
         filled = jnp.sum(hit, axis=1, keepdims=True) > 0.5
         chunk3 = jnp.where(filled, data, EMPTY).astype(BF)
-        more = part_call(scalars, exchange(chunk3), enc_weight, dec_weight, bias_row, offset_row)
-        mine = mine + lax.dynamic_index_in_dim(more, core, 0, keepdims=False)
-        more = lax.dynamic_index_in_dim(more, 1 - core, 0, keepdims=False)
-        return mine, (other.astype(F32) + more).astype(BF), jnp.zeros((), F32)
+        more, more_other = part_call(scalars, exchange(chunk3), *operands)
+        return mine + more, (other.astype(F32) + more_other).astype(BF), jnp.zeros((), F32)
 
     mine, other, unused = lax.while_loop(
         lambda carry: carry[2] > 0.5, rest, (mine, other, flags.reshape(()))
     )
-    swapped = lax.ppermute(other, "tok", [(i, i ^ 1) for i in range(groups)])
-    summed = (mine + swapped.astype(F32)).astype(BF)
+    summed = (mine + swap(other).astype(F32)).astype(BF)
     terms = lax.all_to_all(
         summed,
         "tok",

time: 166 us -> 164 us (0.988)
  Pallas kernels: 31.7 us -> 27.6 us
  other arithmetic: 2.23 us -> 5.63 us
    all_to_all x2, waiting for transfers between devices: 58.6 us -> 52.8 us  [exchange(): lax.all_to_all(shaped, ('tok', 'lat'), split_axis=0, concat_axis=0, tiled...]
    ppermute x1 -> x2, waiting for transfers between devices: 2.65 us -> 7 us  [swap(): return lax.ppermute(values, 'tok', [(i, i ^ 1) for i in range(groups)])]
    pallas_call x2, Pallas kernels: 20.3 us -> 16.3 us  [the longest x1 8.26 us: on_device(): mine1, other1 = part_call(scalars, got1, *operands)]
    add x0 -> x1, other arithmetic: none -> 3.38 us  [on_device(): prior = mine1 + swap(other1)]
  transfers between devices with their start and end apart: 3 -> 4, of which waited for: 3 -> 4; matrix products, arithmetic and copies ran while one was open for 0% -> 2% of each run, Pallas kernels for 10% -> 9%
where the time goes in v2:
time: 164 us; the launch traced here: 163 us
  waiting for transfers between devices  59.8 us (36%)
  blocking collectives  48.1 us (29%)
  Pallas kernels  27.6 us (17%)
  starting transfers between devices  19.5 us (12%)
  other arithmetic  5.63 us (3%)
    all_to_all x2, waiting for transfers between devices, exchange(): lax.all_to_all(shaped, ('tok', 'lat'), split_axis=0, concat_axis=0, tiled...  52.8 us
    all_to_all x1, blocking collectives, on_device(): lax.all_to_all(summed, 'tok', split_axis=0, concat_axis=0, tiled=True, ax...  19.4 us
    all_to_all x2, starting transfers between devices, exchange(): lax.all_to_all(shaped, ('tok', 'lat'), split_axis=0, concat_axis=0, tiled...  19.3 us
    all_gather x1, blocking collectives, on_device(): loans_a = lax.all_gather(lent_a, 'tok', tiled=True)  15.3 us
    all_gather x1, blocking collectives, on_device(): loans_b = lax.all_gather(lent_b, 'tok', tiled=True)  13.5 us
    pallas_call x1, Pallas kernels, on_device(): mine1, other1 = part_call(scalars, got1, *operands)  8.26 us
    pallas_call x1, Pallas kernels, on_device(): pl.pallas_call(functools.partial(chunk_kernel, True), out_shape=[jax.Shap...  8.03 us
    ppermute x2, waiting for transfers between devices, swap(): return lax.ppermute(values, 'tok', [(i, i ^ 1) for i in range(groups)])  7 us
  transfers between devices with their start and end apart: 4, of which 4 were waited for; matrix products, arithmetic and copies ran while one was open for 2% of the time, Pallas kernels for 9%

profile of v2, /device:TPU:6, one launch (start us, length us, event | category | flops | bytes accessed | tf_op | source)
XLA Modules:
  0.0 163.4 jit_solution(8214406742739648502)
XLA Ops:
  0.6 0.0 copy-start
  0.6 4.4 %first_slots.1 = bf16[512,2048]{1,0:T(8,128)(2,1)} custom-call(s32[1,128]{1,0:T(1,128)} %bitcast.22, s32[1,64]{1,0:T(1,128)} %bitcast.24, bf16[128,8192]{1,0:T(8,128)(2,1)} %tokens_in.1), custom_call_target="tpu_custom_call" | custom-call | flops 1073741824 | bytes 5242880 | tf_op jit(solution)/shard_map/first_slots/pallas_call | solution.py:404
  5.0 0.0 copy-start.1
  5.0 0.0 copy-start.2
  5.1 0.0 copy-start.3
  5.1 13.3 %all-to-all-start.2 = ((bf16[64,8,2048]{2,1,0:T(8,128)(2,1)}), bf16[64,8,2048]{2,1,0:T(8,128)(2,1)}, u32[]{:S(2)}, u32[]{:S(2)}) async-start(bf16[64,8,2048]{2,1,0:T(8,128)(2,1)} %bitcast.26), calls=%async_computation.2 | async-start | bytes 4194304 | tf_op jit(solution)/shard_map/all_to_all | solution.py:431
  18.4 0.0 copy-done.1
  18.4 0.0 copy-done.2
  18.4 0.0 copy-done.3
  18.4 1.1 lent_rows.1
  19.5 15.3 %all_gather.6.loans_a = bf16[448,1024]{1,0:T(8,128)(2,1)S(1)} all-gather(bf16[56,1024]{1,0:T(8,128)(2,1)S(1)} %get-tuple-element.67), channel_id=1, replica_groups=mesh['tok'=8,'lat'=32] {'tok'}, dimensions={0}, use_global_device_ids=true | all-gather | bytes 1032192 | tf_op jit(solution)/shard_map/all_gather | solution.py:441
  34.8 13.5 %all_gather.7.loans_b = bf16[448,1024]{1,0:T(8,128)(2,1)S(1)} all-gather(bf16[56,1024]{1,0:T(8,128)(2,1)S(1)} %get-tuple-element.70), channel_id=1, replica_groups=mesh['tok'=8,'lat'=32] {'tok'}, dimensions={0}, use_global_device_ids=true | all-gather | bytes 1032192 | tf_op jit(solution)/shard_map/all_gather | solution.py:443
  48.3 5.9 %second_slots.1 = (bf16[512,2176]{1,0:T(8,128)(2,1)}, s32[8,128]{1,0:T(8,128)S(1)}) custom-call(s32[1]{0:T(128)} %bitcast.5.group, bf16[128,8192]{1,0:T(8,128)(2,1)S(1)} %copy-done.3, bf16[448,1024]{1,0:T(8,128)(2,1)S(1)} %all_gather.6.loans_a, bf16[448,1024]{1,0:T(8,128)(2,1)S(1)} %all_gather.7.loans_b), custom_call_target="tpu_custom_call" | custom-call | flops 1073741824 | bytes 5242880 | tf_op jit(solution)/shard_map/second_slots/pallas_call | solution.py:445
  54.2 15.5 %all-to-all-done.2 = bf16[64,8,2048]{2,1,0:T(8,128)(2,1)} async-done(((bf16[64,8,2048]{2,1,0:T(8,128)(2,1)}), bf16[64,8,2048]{2,1,0:T(8,128)(2,1)}, u32[]{:S(2)}, u32[]{:S(2)}) %all-to-all-start.2) | async-done | bytes 2097184 | tf_op jit(solution)/shard_map/all_to_all | solution.py:431
  69.7 0.0 copy-start.7
  69.7 6.0 %all-to-all-start.1 = ((bf16[64,8,2176]{2,1,0:T(8,128)(2,1)}), bf16[64,8,2176]{2,1,0:T(8,128)(2,1)}, u32[]{:S(2)}, u32[]{:S(2)}) async-start(bf16[64,8,2176]{2,1,0:T(8,128)(2,1)} %bitcast.8), calls=%async_computation.1 | async-start | bytes 4456448 | tf_op jit(solution)/shard_map/all_to_all | solution.py:431
  75.7 0.0 copy-done
  75.7 0.1 dynamic-slice_bitcast_fusion
  75.8 0.1 copy.16.bias
  75.9 0.1 pad_add_fusion.at
  75.9 0.0 copy-done.7
  75.9 8.3 %chunk_gradients.3 = (f32[4,128,1024]{2,1,0:T(8,128)}, f32[4,128,1024]{2,1,0:T(8,128)}) custom-call(s32[2]{0:T(128)S(1)} %pad_add_fusion.at, bf16[512,2048]{1,0:T(8,128)(2,1)} %bitcast.13.chunk_in, bf16[128,8192]{1,0:T(8,128)(2,1)} %enc_in.3, bf16[128,8192]{1,0:T(8,128)(2,1)} %dec_in.3, f32[64,1]{1,0:T(8,128)S(1)} %copy.16.bias, f32[1,8192]{1,0:T(1,128)S(1)} %bitcast.30), custom_call_target="tpu_custom_call" | custom-call | flops 2684354560 | bytes 12582912 | tf_op jit(solution)/shard_map/chunk_gradients/pallas_call | solution.py:490
  84.2 0.1 collective-permute-start
  84.3 4.4 %collective-permute-done = f32[4,128,1024]{2,1,0:T(8,128)S(1)} collective-permute-done((f32[4,128,1024]{2,1,0:T(8,128)}, f32[4,128,1024]{2,1,0:T(8,128)S(1)}, u32[]{:S(2)}, u32[]{:S(2)}) %collective-permute-start) | collective-permute-done | bytes 2097184 | tf_op jit(solution)/shard_map/ppermute | solution.py:477
  88.7 3.4 %add.112.refs_0_ = f32[4,128,1024]{2,1,0:T(8,128)} add(f32[4,128,1024]{2,1,0:T(8,128)} %get-tuple-element.72, f32[4,128,1024]{2,1,0:T(8,128)S(1)} %collective-permute-done) | non-fusion elementwise | flops 524288 | bytes 6291456 | tf_op jit(solution)/shard_map/add | solution.py:491
  92.1 37.3 %all-to-all-done.1 = bf16[64,8,2176]{2,1,0:T(8,128)(2,1)} async-done(((bf16[64,8,2176]{2,1,0:T(8,128)(2,1)}), bf16[64,8,2176]{2,1,0:T(8,128)(2,1)}, u32[]{:S(2)}, u32[]{:S(2)}) %all-to-all-start.1) | async-done | bytes 2228256 | tf_op jit(solution)/shard_map/all_to_all | solution.py:431
  129.4 8.0 %last_gradients.1 = (f32[4,128,1024]{2,1,0:T(8,128)}, bf16[4,128,1024]{2,1,0:T(8,128)(2,1)S(1)}, f32[1]{0:T(128)}) custom-call(s32[2]{0:T(128)S(1)} %pad_add_fusion.at, bf16[512,2176]{1,0:T(8,128)(2,1)} %bitcast.9.chunk_in, bf16[128,8192]{1,0:T(8,128)(2,1)} %enc_in.3, bf16[128,8192]{1,0:T(8,128)(2,1)} %dec_in.3, f32[64,1]{1,0:T(8,128)S(1)} %copy.16.bias, ...), custom_call_target="tpu_custom_call" | custom-call | flops 2684354560 | bytes 12582912 | tf_op jit(solution)/shard_map/last_gradients/pallas_call | solution.py:492
  137.4 0.7 while.11
  138.1 0.1 collective-permute-start.1
  138.2 2.6 %collective-permute-done.1 = bf16[4,128,1024]{2,1,0:T(8,128)(2,1)S(1)} collective-permute-done((bf16[4,128,1024]{2,1,0:T(8,128)(2,1)S(1)}, bf16[4,128,1024]{2,1,0:T(8,128)(2,1)S(1)}, u32[]{:S(2)}, u32[]{:S(2)}) %collective-permute-start.1) | collective-permute-done | bytes 1048608 | tf_op jit(solution)/shard_map/ppermute | solution.py:477
  140.8 2.0 %add_convert_fusion.1 = bf16[4,128,1024]{2,1,0:T(8,128)(2,1)S(1)} fusion(f32[4,128,1024]{2,1,0:T(8,128)} %get-tuple-element.78, bf16[4,128,1024]{2,1,0:T(8,128)(2,1)S(1)} %collective-permute-done.1), kind=kLoop, calls=%fused_computation.72 | loop fusion | flops 1572864 | bytes 4194304 | tf_op jit(solution)/shard_map/convert_element_type | solution.py:527
  142.8 19.4 %all_to_all.19 = bf16[4,128,1024]{2,1,0:T(8,128)(2,1)S(1)} all-to-all(bf16[4,128,1024]{2,1,0:T(8,128)(2,1)S(1)} %add_convert_fusion.1), channel_id=1, replica_groups={{0,64,128,192},{32,96,160,224},{1,65,129,193},{33,97,161,225},{2,66,130..., dimensions={0} | all-to-all | bytes 2097152 | tf_op jit(solution)/shard_map/all_to_all | solution.py:528
  162.1 0.2 convert_reduce_fusion
  162.4 1.1 fusion.51
Async XLA Ops:
  0.6 75.1 %copy-start = (f32[128]{0:T(128)S(1)}, f32[128]{0:T(128)}, u32[]{:S(2)}) copy-start(f32[128]{0:T(128)} %param.12) | copy-start | bytes 1540
  5.0 13.4 %copy-start.1 = (s32[128,1]{0,1:T(1,128)S(1)}, s32[128,1]{0,1:T(1,128)}, u32[]{:S(2)}) copy-start(s32[128,1]{0,1:T(1,128)} %param.14) | copy-start | bytes 1540
  5.0 13.4 %copy-start.2 = (s32[64]{0:T(128)S(1)}, s32[64]{0:T(128)}, u32[]{:S(2)}) copy-start(s32[64]{0:T(128)} %param.15) | copy-start | bytes 772
  5.1 13.4 %copy-start.3 = (bf16[128,8192]{1,0:T(8,128)(2,1)S(1)}, bf16[128,8192]{1,0:T(8,128)(2,1)}, u32[]{:S(2)}) copy-start(bf16[128,8192]{1,0:T(8,128)(2,1)} %tokens_in.1) | copy-start | bytes 6291460
  5.1 64.6 %all-to-all-start.2 = ((bf16[64,8,2048]{2,1,0:T(8,128)(2,1)}), bf16[64,8,2048]{2,1,0:T(8,128)(2,1)}, u32[]{:S(2)}, u32[]{:S(2)}) async-start(bf16[64,8,2048]{2,1,0:T(8,128)(2,1)} %bitcast.26), calls=%async_computation.2 | async-start | bytes 4194304 | tf_op jit(solution)/shard_map/all_to_all | solution.py:431
  69.7 6.3 %copy-start.7 = (f32[8192]{0:T(1024)S(1)}, f32[8192]{0:T(1024)}, u32[]{:S(2)}) copy-start(f32[8192]{0:T(1024)} %param.10) | copy-start | bytes 98308
  69.7 59.7 %all-to-all-start.1 = ((bf16[64,8,2176]{2,1,0:T(8,128)(2,1)}), bf16[64,8,2176]{2,1,0:T(8,128)(2,1)}, u32[]{:S(2)}, u32[]{:S(2)}) async-start(bf16[64,8,2176]{2,1,0:T(8,128)(2,1)} %bitcast.8), calls=%async_computation.1 | async-start | bytes 4456448 | tf_op jit(solution)/shard_map/all_to_all | solution.py:431
  84.2 4.5 %collective-permute-start = (f32[4,128,1024]{2,1,0:T(8,128)}, f32[4,128,1024]{2,1,0:T(8,128)S(1)}, u32[]{:S(2)}, u32[]{:S(2)}) collective-permute-start(f32[4,128,1024]{2,1,0:T(8,128)} %get-tuple-element.73), channel_id=1, source_target_pairs={{0,32},{32,0},{64,96},{96,64},{128,160},{160,128},{192,224},{224,1... | collective-permute-start | bytes 6291464 | tf_op jit(solution)/shard_map/ppermute | solution.py:477
  138.1 2.7 %collective-permute-start.1 = (bf16[4,128,1024]{2,1,0:T(8,128)(2,1)S(1)}, bf16[4,128,1024]{2,1,0:T(8,128)(2,1)S(1)}, u32[]{:S(2)}, u32[]{:S(2)}) collective-permute-start(bf16[4,128,1024]{2,1,0:T(8,128)(2,1)S(1)} %get-tuple-element.79), channel_id=1, source_target_pairs={{0,32},{32,0},{64,96},{96,64},{128,160},{160,128},{192,224},{224,1... | collective-permute-start | bytes 3145736 | tf_op jit(solution)/shard_map/ppermute | solution.py:477

commit v3 on v2

--- a/solution.py
+++ b/solution.py
@@ -17,7 +17,6 @@
 GROUP = CUTS * SLOTS
 STRIDE = 8
 EMPTY = 2.0**100
-EXTRA = 128
 STEP = 1024
 PIECES = 8
 LENT = (6, 7)
@@ -133,7 +132,7 @@
         first += count
 
 
-def second_kernel(targets, group, tokens, loans_a, loans_b, chunk, left):
+def second_kernel(targets, group, tokens, loans_a, loans_b, chunk, left, flags):
     rows, width = tokens.shape
     part = width // CUTS
     lines = (LENT[0] + 1) * PIECES
@@ -200,7 +199,7 @@
     hit_b = flat(codes == codes_of_lines(LENT[0], LENT[1]))
     filled = jnp.sum(hit, axis=1, keepdims=True) + jnp.sum(hit_a, axis=1, keepdims=True)
     filled = filled + jnp.sum(hit_b, axis=1, keepdims=True) > 0.5
-    chunk[:, part:] = jnp.broadcast_to(flag, (hit.shape[0], EXTRA)).astype(BF)
+    flags[...] = jnp.broadcast_to(flag, flags.shape)
     per_cut = part // STEP
     piece = iota((1, size), 1) % PIECES
     for i in range(per_cut):
@@ -312,15 +311,13 @@
     refs = list(refs)
     prior_in = refs.pop(0) if with_prior else None
     mine_out, other_out = refs.pop(0), refs.pop(0)
-    flags = refs.pop(0) if with_prior else None
     chunk, enc, dec, cent, err, acc, sems, mine, other, sems_out = refs[:10]
     latents = enc.shape[0]
     core = at[0]
     ready = Loader(sems, at[1], chunk_in, enc_in, dec_in, chunk, enc, dec)
     if with_prior:
-        prior, marks = refs[10:]
+        prior = refs[10]
         ready.move("third", prior_in, prior)
-        ready.move("marks", chunk_in.at[:, pl.ds(chunk.shape[1], EXTRA)], marks)
 
     def out_copy(which, grad):
         source, result = ((mine, mine_out), (other, other_out))[which]
@@ -345,9 +342,6 @@
             out_copy(1, grad).start()
 
     gradient_body(chunk, enc, dec, bias, dec_bias, cent, err, acc, store, ready)
-    if with_prior:
-        ready("marks", 0)
-        flags[0] = jnp.max(marks[...].astype(F32))
     for which in range(2):
         for grad in range(2):
             out_copy(which, grad).wait()
@@ -442,19 +436,28 @@
     loans_a, lent_b = lax.optimization_barrier((loans_a, lent_b))
     loans_b = lax.all_gather(lent_b, "tok", tiled=True)
     got1 = exchange(chunk1)
-    chunk2, left = pl.pallas_call(
+    chunk2, left, flags = pl.pallas_call(
         functools.partial(second_kernel, targets),
         out_shape=[
-            jax.ShapeDtypeStruct((slot_rows, part + EXTRA), BF),
+            chunk_shape,
             jax.ShapeDtypeStruct((8, rows), I32),
+            jax.ShapeDtypeStruct((8, rows), F32),
         ],
         in_specs=[smem()] + [vmem()] * 3,
-        out_specs=[vmem()] * 2,
+        out_specs=[vmem()] * 3,
         compiler_params=room(24),
         cost_estimate=move_cost,
         name="second_slots",
     )(me.reshape(1), tokens, loans_a, loans_b)
     got2 = exchange(chunk2)
+    line = 4
+    along_x = [[i * line + j for j in range(line)] for i in range(lat_count // line)]
+    along_z = [[i * line + j for i in range(lat_count // line)] for j in range(line)]
+
+    def highest(values, lines):
+        return jnp.max(lax.all_gather(values, "lat", axis_index_groups=lines), axis=0)
+
+    flags = highest(flags, along_x)
     bias_row = lax.dynamic_slice_in_dim(enc_bias, first_row, latents).reshape(latents, 1)
     offset_row = dec_bias.reshape(1, width)
     half_shape = (CUTS, 2 * latents, STEP)
@@ -488,28 +491,39 @@
         name="chunk_gradients",
     )
     mine1, other1 = part_call(scalars, got1, *operands)
+    other1, flags = lax.optimization_barrier((other1, flags))
     prior = mine1 + swap(other1)
-    mine, other, flags = pl.pallas_call(
+    mine, other = pl.pallas_call(
         functools.partial(chunk_kernel, True),
         out_shape=[
             jax.ShapeDtypeStruct(half_shape, F32),
             jax.ShapeDtypeStruct(half_shape, BF),
-            jax.ShapeDtypeStruct((1,), F32),
         ],
         in_specs=[smem(), anywhere()] + [hbm()] * 2 + [vmem()] * 2 + [hbm()],
-        out_specs=[anywhere()] * 2 + [smem()],
+        out_specs=[anywhere()] * 2,
         scratch_shapes=[
             *work(BF),
             pltpu.VMEM(half_shape, F32),
-            pltpu.VMEM((slot_rows, EXTRA), BF),
         ],
         compiler_params=room(56),
         cost_estimate=matmul_cost,
         name="last_gradients",
     )(scalars, got2, *operands, prior)
 
+    def gradients(summed):
+        terms = lax.all_to_all(
+            summed,
+            "tok",
+            split_axis=0,
+            concat_axis=0,
+            tiled=True,
+            axis_index_groups=[[2 * i + c for i in range(chips)] for c in range(2)],
+        )
+        total = jnp.sum(terms.astype(F32).reshape(chips // 2, 2, 2, latents, STEP), axis=0)
+        return total[:, 0].reshape(2 * latents, STEP), total[:, 1].reshape(2 * latents, STEP)
+
     def rest(carry):
-        mine, other, unused = carry
+        enc_grad, dec_grad, unused = carry
         codes, cut = slot_codes(targets, DIRECT)
         hit = flat(codes == left[:1])
         data = jnp.zeros((slot_rows, part), F32)
@@ -519,22 +533,17 @@
         filled = jnp.sum(hit, axis=1, keepdims=True) > 0.5
         chunk3 = jnp.where(filled, data, EMPTY).astype(BF)
         more, more_other = part_call(scalars, exchange(chunk3), *operands)
-        return mine + more, (other.astype(F32) + more_other).astype(BF), jnp.zeros((), F32)
-
-    mine, other, unused = lax.while_loop(
-        lambda carry: carry[2] > 0.5, rest, (mine, other, flags.reshape(()))
+        enc_more, dec_more = gradients((more + swap(more_other)).astype(BF))
+        return enc_grad + enc_more, dec_grad + dec_more, jnp.zeros((), F32)
+
+    summed = (mine + swap(other).astype(F32)).astype(BF)
+    summed, flags = lax.optimization_barrier((summed, flags))
+    enc_grad, dec_grad = gradients(summed)
+    flags = highest(flags, along_z)
+    enc_grad, dec_grad, unused = lax.while_loop(
+        lambda carry: carry[2] > 0.5, rest, (enc_grad, dec_grad, flags[0, 0])
     )
-    summed = (mine + swap(other).astype(F32)).astype(BF)
-    terms = lax.all_to_all(
-        summed,
-        "tok",
-        split_axis=0,
-        concat_axis=0,
-        tiled=True,
-        axis_index_groups=[[2 * i + c for i in range(chips)] for c in range(2)],
-    )
-    total = jnp.sum(terms.astype(F32).reshape(chips // 2, 2, 2, latents, STEP), axis=0)
-    return total[:, 0].reshape(2 * latents, STEP), total[:, 1].reshape(2 * latents, STEP)
+    return enc_grad, dec_grad
 
 
 def solution(mesh):

time: 164 us -> 173 us (1.055)
  blocking collectives: 48.1 us -> 65.3 us
  waiting for transfers between devices: 59.8 us -> 45.3 us
  starting transfers between devices: 19.5 us -> 23.6 us
    all_gather x0 -> x2, blocking collectives: none -> 36.5 us  [highest(): lax.all_gather(values, 'lat', axis_index_groups=lines)]
    all_to_all x1 -> x0, blocking collectives: 19.4 us -> none  [on_device(): lax.all_to_all(summed, 'tok', split_axis=0, concat_axis=0, tiled=True, ax...]
    all_to_all x2, waiting for transfers between devices: 52.8 us -> 38 us  [exchange(): lax.all_to_all(shaped, ('tok', 'lat'), split_axis=0, concat_axis=0, tiled...]
    all_to_all x0 -> x1, starting transfers between devices: none -> 4.17 us  [gradients(): lax.all_to_all(summed, 'tok', split_axis=0, concat_axis=0, tiled=True, ax...]
  transfers between devices with their start and end apart: 4 -> 5, of which waited for: 4 -> 4; matrix products, arithmetic and copies ran while one was open for 2% -> 2% of each run, Pallas kernels for 9% -> 9%
where the time goes in v3:
time: 173 us; the launch traced here: 172 us
  blocking collectives  65.3 us (38%)
  waiting for transfers between devices  45.3 us (26%)
  Pallas kernels  27.6 us (16%)
  starting transfers between devices  23.6 us (14%)
  other arithmetic  6.58 us (4%)
  local copies, waits for them, and re-layouts  1.77 us (1%)
    all_to_all x2, waiting for transfers between devices, exchange(): lax.all_to_all(shaped, ('tok', 'lat'), split_axis=0, concat_axis=0, tiled...  38 us
    all_gather x2, blocking collectives, highest(): lax.all_gather(values, 'lat', axis_index_groups=lines)  36.5 us
    all_to_all x2, starting transfers between devices, exchange(): lax.all_to_all(shaped, ('tok', 'lat'), split_axis=0, concat_axis=0, tiled...  19.3 us
    all_gather x1, blocking collectives, on_device(): loans_a = lax.all_gather(lent_a, 'tok', tiled=True)  15.3 us
    all_gather x1, blocking collectives, on_device(): loans_b = lax.all_gather(lent_b, 'tok', tiled=True)  13.5 us
    pallas_call x1, Pallas kernels, on_device(): mine1, other1 = part_call(scalars, got1, *operands)  8.27 us
    pallas_call x1, Pallas kernels, on_device(): pl.pallas_call(functools.partial(chunk_kernel, True), out_shape=[jax.Shap...  8.07 us
    ppermute x2, waiting for transfers between devices, swap(): return lax.ppermute(values, 'tok', [(i, i ^ 1) for i in range(groups)])  7.22 us
  transfers between devices with their start and end apart: 5, of which 4 were waited for; matrix products, arithmetic and copies ran while one was open for 2% of the time, Pallas kernels for 9%

profile of v3, /device:TPU:6, one launch (start us, length us, event | category | flops | bytes accessed | tf_op | source)
XLA Modules:
  0.0 172.0 jit_solution(14147090114855197254)
XLA Ops:
  0.6 0.0 copy-start
  0.6 4.4 %first_slots.1 = bf16[512,2048]{1,0:T(8,128)(2,1)} custom-call(s32[1,128]{1,0:T(1,128)} %bitcast.32, s32[1,64]{1,0:T(1,128)} %bitcast.34, bf16[128,8192]{1,0:T(8,128)(2,1)} %tokens_in.1), custom_call_target="tpu_custom_call" | custom-call | flops 1073741824 | bytes 5242880 | tf_op jit(solution)/shard_map/first_slots/pallas_call | solution.py:398
  5.0 0.0 copy-start.1
  5.0 0.0 copy-start.2
  5.1 0.0 copy-start.3
  5.1 13.3 %all-to-all-start.3 = ((bf16[64,8,2048]{2,1,0:T(8,128)(2,1)}), bf16[64,8,2048]{2,1,0:T(8,128)(2,1)}, u32[]{:S(2)}, u32[]{:S(2)}) async-start(bf16[64,8,2048]{2,1,0:T(8,128)(2,1)} %bitcast.40), calls=%async_computation.3 | async-start | bytes 4194304 | tf_op jit(solution)/shard_map/all_to_all | solution.py:425
  18.4 0.0 copy-done.1
  18.4 0.0 copy-done.2
  18.4 0.0 copy-done.3
  18.4 1.1 lent_rows.1
  19.5 15.3 %all_gather.18.loans_a = bf16[448,1024]{1,0:T(8,128)(2,1)S(1)} all-gather(bf16[56,1024]{1,0:T(8,128)(2,1)S(1)} %get-tuple-element.71), channel_id=1, replica_groups=mesh['tok'=8,'lat'=32] {'tok'}, dimensions={0}, use_global_device_ids=true | all-gather | bytes 1032192 | tf_op jit(solution)/shard_map/all_gather | solution.py:435
  34.8 13.5 %all_gather.19.loans_b = bf16[448,1024]{1,0:T(8,128)(2,1)S(1)} all-gather(bf16[56,1024]{1,0:T(8,128)(2,1)S(1)} %get-tuple-element.74), channel_id=1, replica_groups=mesh['tok'=8,'lat'=32] {'tok'}, dimensions={0}, use_global_device_ids=true | all-gather | bytes 1032192 | tf_op jit(solution)/shard_map/all_gather | solution.py:437
  48.3 5.8 %second_slots.1 = (bf16[512,2048]{1,0:T(8,128)(2,1)}, s32[8,128]{1,0:T(8,128)S(1)}, f32[8,128]{1,0:T(8,128)S(1)}) custom-call(s32[1]{0:T(128)} %bitcast.8.group, bf16[128,8192]{1,0:T(8,128)(2,1)S(1)} %copy-done.3, bf16[448,1024]{1,0:T(8,128)(2,1)S(1)} %all_gather.18.loans_a, bf16[448,1024]{1,0:T(8,128)(2,1)S(1)} %all_gather.19.loans_b), custom_call_target="tpu_custom_call" | custom-call | flops 1073741824 | bytes 5242880 | tf_op jit(solution)/shard_map/second_slots/pallas_call | solution.py:439
  54.1 15.6 %all-to-all-done.3 = bf16[64,8,2048]{2,1,0:T(8,128)(2,1)} async-done(((bf16[64,8,2048]{2,1,0:T(8,128)(2,1)}), bf16[64,8,2048]{2,1,0:T(8,128)(2,1)}, u32[]{:S(2)}, u32[]{:S(2)}) %all-to-all-start.3) | async-done | bytes 2097184 | tf_op jit(solution)/shard_map/all_to_all | solution.py:425
  69.7 0.0 copy-start.10
  69.7 6.0 %all-to-all-start.2 = ((bf16[64,8,2048]{2,1,0:T(8,128)(2,1)}), bf16[64,8,2048]{2,1,0:T(8,128)(2,1)}, u32[]{:S(2)}, u32[]{:S(2)}) async-start(bf16[64,8,2048]{2,1,0:T(8,128)(2,1)} %bitcast.11), calls=%async_computation.2 | async-start | bytes 4194304 | tf_op jit(solution)/shard_map/all_to_all | solution.py:425
  75.7 0.0 copy-done
  75.7 0.1 dynamic-slice_bitcast_fusion
  75.8 0.1 copy.16.bias
  75.9 12.0 %all-gather = f32[32,128]{1,0:T(8,128)S(1)} all-gather(f32[8,128]{1,0:T(8,128)S(1)} %get-tuple-element.78), channel_id=2, replica_groups={{0,1,2,3},{4,5,6,7},{8,9,10,11},{12,13,14,15},{16,17,18,19},{20,21,22,2..., dimensions={0}, use_global_device_ids=true | all-gather | bytes 20480 | tf_op jit(solution)/shard_map/all_gather | solution.py:458
  87.9 0.1 pad_add_fusion.at
  88.0 0.0 copy-done.10
  88.0 8.3 %chunk_gradients.3 = (f32[4,128,1024]{2,1,0:T(8,128)}, f32[4,128,1024]{2,1,0:T(8,128)}) custom-call(s32[2]{0:T(128)S(1)} %pad_add_fusion.at, bf16[512,2048]{1,0:T(8,128)(2,1)} %bitcast.16.chunk_in, bf16[128,8192]{1,0:T(8,128)(2,1)} %enc_in.3, bf16[128,8192]{1,0:T(8,128)(2,1)} %dec_in.3, f32[64,1]{1,0:T(8,128)S(1)} %copy.16.bias, f32[1,8192]{1,0:T(1,128)S(1)} %bitcast.42), custom_call_target="tpu_custom_call" | custom-call | flops 2684354560 | bytes 12582912 | tf_op jit(solution)/shard_map/chunk_gradients/pallas_call | solution.py:493
  96.3 0.1 collective-permute-start.1
  96.4 4.4 %collective-permute-done.1 = f32[4,128,1024]{2,1,0:T(8,128)S(1)} collective-permute-done((f32[4,128,1024]{2,1,0:T(8,128)}, f32[4,128,1024]{2,1,0:T(8,128)S(1)}, u32[]{:S(2)}, u32[]{:S(2)}) %collective-permute-start.1) | collective-permute-done | bytes 2097184 | tf_op jit(solution)/shard_map/ppermute | solution.py:480
  100.8 3.4 %add.115.refs_0_ = f32[4,128,1024]{2,1,0:T(8,128)} add(f32[4,128,1024]{2,1,0:T(8,128)} %get-tuple-element.76, f32[4,128,1024]{2,1,0:T(8,128)S(1)} %collective-permute-done.1) | non-fusion elementwise | flops 524288 | bytes 6291456 | tf_op jit(solution)/shard_map/add | solution.py:495
  104.1 22.4 %all-to-all-done.2 = bf16[64,8,2048]{2,1,0:T(8,128)(2,1)} async-done(((bf16[64,8,2048]{2,1,0:T(8,128)(2,1)}), bf16[64,8,2048]{2,1,0:T(8,128)(2,1)}, u32[]{:S(2)}, u32[]{:S(2)}) %all-to-all-start.2) | async-done | bytes 2097184 | tf_op jit(solution)/shard_map/all_to_all | solution.py:425
  126.6 8.1 %last_gradients.1 = (f32[4,128,1024]{2,1,0:T(8,128)}, bf16[4,128,1024]{2,1,0:T(8,128)(2,1)}) custom-call(s32[2]{0:T(128)S(1)} %pad_add_fusion.at, bf16[512,2048]{1,0:T(8,128)(2,1)} %bitcast.12.chunk_in, bf16[128,8192]{1,0:T(8,128)(2,1)} %enc_in.3, bf16[128,8192]{1,0:T(8,128)(2,1)} %dec_in.3, f32[64,1]{1,0:T(8,128)S(1)} %copy.16.bias, ...), custom_call_target="tpu_custom_call" | custom-call | flops 2684354560 | bytes 12582912 | tf_op jit(solution)/shard_map/last_gradients/pallas_call | solution.py:496
  134.6 0.1 collective-permute-start.2
  134.7 2.9 %collective-permute-done.2 = bf16[4,128,1024]{2,1,0:T(8,128)(2,1)S(1)} collective-permute-done((bf16[4,128,1024]{2,1,0:T(8,128)(2,1)}, bf16[4,128,1024]{2,1,0:T(8,128)(2,1)S(1)}, u32[]{:S(2)}, u32[]{:S(2)}) %collective-permute-start.2) | collective-permute-done | bytes 1048608 | tf_op jit(solution)/shard_map/ppermute | solution.py:480
  137.6 2.9 %add_convert_fusion.1 = bf16[4,128,1024]{2,1,0:T(8,128)(2,1)} fusion(f32[4,128,1024]{2,1,0:T(8,128)} %get-tuple-element.80, bf16[4,128,1024]{2,1,0:T(8,128)(2,1)S(1)} %collective-permute-done.2), kind=kLoop, calls=%fused_computation.75 | loop fusion | flops 1572864 | bytes 4194304 | tf_op jit(solution)/shard_map/convert_element_type | solution.py:539
  140.5 4.2 %all-to-all-start.4 = ((bf16[4,128,1024]{2,1,0:T(8,128)(2,1)}), bf16[4,128,1024]{2,1,0:T(8,128)(2,1)S(1)}, u32[]{:S(2)}, u32[]{:S(2)}) async-start(bf16[4,128,1024]{2,1,0:T(8,128)(2,1)} %add_convert_fusion.1), calls=%async_computation.4 | async-start | bytes 2097152 | tf_op jit(solution)/shard_map/all_to_all | solution.py:514
  144.7 24.5 %all-gather.1 = f32[64,128]{1,0:T(8,128)S(1)} all-gather(f32[8,128]{1,0:T(8,128)S(1)} %bitcast_reduce_fusion.1), channel_id=3, replica_groups={{0,4,8,12,16,20,24,28},{1,5,9,13,17,21,25,29},{2,6,10,14,18,22,26,30},{..., dimensions={0}, use_global_device_ids=true | all-gather | bytes 36864 | tf_op jit(solution)/shard_map/all_gather | solution.py:458
  169.2 0.5 slice.32
  169.7 0.0 all-to-all-done.4
  169.7 0.2 convert_reduce_fusion.1
  169.9 1.0 fusion.52
  170.9 0.8 while.11
  (2 shorter events, 0.0 us)
Async XLA Ops:
  0.6 75.1 %copy-start = (f32[128]{0:T(128)S(1)}, f32[128]{0:T(128)}, u32[]{:S(2)}) copy-start(f32[128]{0:T(128)} %param.12) | copy-start | bytes 1540
  5.0 13.4 %copy-start.1 = (s32[128,1]{0,1:T(1,128)S(1)}, s32[128,1]{0,1:T(1,128)}, u32[]{:S(2)}) copy-start(s32[128,1]{0,1:T(1,128)} %param.14) | copy-start | bytes 1540
  5.0 13.4 %copy-start.2 = (s32[64]{0:T(128)S(1)}, s32[64]{0:T(128)}, u32[]{:S(2)}) copy-start(s32[64]{0:T(128)} %param.15) | copy-start | bytes 772
  5.1 13.4 %copy-start.3 = (bf16[128,8192]{1,0:T(8,128)(2,1)S(1)}, bf16[128,8192]{1,0:T(8,128)(2,1)}, u32[]{:S(2)}) copy-start(bf16[128,8192]{1,0:T(8,128)(2,1)} %tokens_in.1) | copy-start | bytes 6291460
  5.1 64.6 %all-to-all-start.3 = ((bf16[64,8,2048]{2,1,0:T(8,128)(2,1)}), bf16[64,8,2048]{2,1,0:T(8,128)(2,1)}, u32[]{:S(2)}, u32[]{:S(2)}) async-start(bf16[64,8,2048]{2,1,0:T(8,128)(2,1)} %bitcast.40), calls=%async_computation.3 | async-start | bytes 4194304 | tf_op jit(solution)/shard_map/all_to_all | solution.py:425
  69.7 18.3 %copy-start.10 = (f32[8192]{0:T(1024)S(1)}, f32[8192]{0:T(1024)}, u32[]{:S(2)}) copy-start(f32[8192]{0:T(1024)} %param.10) | copy-start | bytes 98308
  69.7 56.9 %all-to-all-start.2 = ((bf16[64,8,2048]{2,1,0:T(8,128)(2,1)}), bf16[64,8,2048]{2,1,0:T(8,128)(2,1)}, u32[]{:S(2)}, u32[]{:S(2)}) async-start(bf16[64,8,2048]{2,1,0:T(8,128)(2,1)} %bitcast.11), calls=%async_computation.2 | async-start | bytes 4194304 | tf_op jit(solution)/shard_map/all_to_all | solution.py:425
  96.3 4.5 %collective-permute-start.1 = (f32[4,128,1024]{2,1,0:T(8,128)}, f32[4,128,1024]{2,1,0:T(8,128)S(1)}, u32[]{:S(2)}, u32[]{:S(2)}) collective-permute-start(f32[4,128,1024]{2,1,0:T(8,128)} %get-tuple-element.79), channel_id=1, source_target_pairs={{0,32},{32,0},{64,96},{96,64},{128,160},{160,128},{192,224},{224,1... | collective-permute-start | bytes 6291464 | tf_op jit(solution)/shard_map/ppermute | solution.py:480
  134.6 3.0 %collective-permute-start.2 = (bf16[4,128,1024]{2,1,0:T(8,128)(2,1)}, bf16[4,128,1024]{2,1,0:T(8,128)(2,1)S(1)}, u32[]{:S(2)}, u32[]{:S(2)}) collective-permute-start(bf16[4,128,1024]{2,1,0:T(8,128)(2,1)} %get-tuple-element.81), channel_id=1, source_target_pairs={{0,32},{32,0},{64,96},{96,64},{128,160},{160,128},{192,224},{224,1... | collective-permute-start | bytes 3145736 | tf_op jit(solution)/shard_map/ppermute | solution.py:480
  140.5 29.2 %all-to-all-start.4 = ((bf16[4,128,1024]{2,1,0:T(8,128)(2,1)}), bf16[4,128,1024]{2,1,0:T(8,128)(2,1)S(1)}, u32[]{:S(2)}, u32[]{:S(2)}) async-start(bf16[4,128,1024]{2,1,0:T(8,128)(2,1)} %add_convert_fusion.1), calls=%async_computation.4 | async-start | bytes 2097152 | tf_op jit(solution)/shard_map/all_to_all | solution.py:514

commit v4 on v2

--- a/solution.py
+++ b/solution.py
@@ -19,6 +19,7 @@
 EMPTY = 2.0**100
 EXTRA = 128
 STEP = 1024
+FINE = 512
 PIECES = 8
 LENT = (6, 7)
 
@@ -64,9 +65,9 @@
     return (places & 1) * (targets // 2) + (places >> 1)
 
 
-def cut_columns(ref, i):
+def cut_columns(ref, i, step=STEP):
     part = ref.shape[1] // CUTS
-    return [ref[:, h * part + i * STEP : h * part + (i + 1) * STEP] for h in range(CUTS)]
+    return [ref[:, h * part + i * step : h * part + (i + 1) * step] for h in range(CUTS)]
 
 
 def places_of(ids, home):
@@ -76,17 +77,26 @@
     return mm(table, named)[:1].astype(I32)
 
 
-def first_kernel(targets, ids, home, tokens_in, chunk_out, tokens, chunk, sems_in, sems_out):
+def first_kernel(
+    targets, ids_in, home_in, tokens_in, chunk_out, ids, home, tokens, chunk, sems_in, sems_out
+):
     rows, width = tokens.shape
     part = width // CUTS
-    steps = part // STEP
+    steps = part // FINE
     loads = []
+
+    def load(source, target):
+        loads.append(pltpu.make_async_copy(source, target, sems_in.at[len(loads)]))
+        loads[-1].start()
+
+    load(ids_in, ids)
+    load(home_in, home)
     for i in range(steps):
         for h in range(CUTS):
-            columns = pl.ds(h * part + i * STEP, STEP)
-            sem = sems_in.at[len(loads)]
-            loads.append(pltpu.make_async_copy(tokens_in.at[:, columns], tokens.at[:, columns], sem))
-            loads[-1].start()
+            columns = pl.ds(h * part + i * FINE, FINE)
+            load(tokens_in.at[:, columns], tokens.at[:, columns])
+    loads[0].wait()
+    loads[1].wait()
     target = target_of(places_of(ids, home), targets)
     unused, rank = ranks_of(target, targets)
     codes, cut = slot_codes(targets, 0)
@@ -97,10 +107,10 @@
     stores = []
     for i in range(steps):
         for h in range(CUTS):
-            loads[i * CUTS + h].wait()
-        got = mm(wide, jnp.concatenate(cut_columns(tokens, i), axis=0))
-        chunk[:, i * STEP : (i + 1) * STEP] = jnp.where(filled, got, EMPTY).astype(BF)
-        columns = pl.ds(i * STEP, STEP)
+            loads[2 + i * CUTS + h].wait()
+        got = mm(wide, jnp.concatenate(cut_columns(tokens, i, FINE), axis=0))
+        chunk[:, i * FINE : (i + 1) * FINE] = jnp.where(filled, got, EMPTY).astype(BF)
+        columns = pl.ds(i * FINE, FINE)
         stores.append(
             pltpu.make_async_copy(chunk.at[:, columns], chunk_out.at[:, columns], sems_out.at[i])
         )
@@ -404,13 +414,15 @@
     chunk1 = pl.pallas_call(
         functools.partial(first_kernel, targets),
         out_shape=chunk_shape,
-        in_specs=[vmem()] * 2 + [anywhere()],
+        in_specs=[anywhere()] * 3,
         out_specs=anywhere(),
         scratch_shapes=[
+            pltpu.VMEM(ids_row.shape, I32),
+            pltpu.VMEM(home_row.shape, I32),
             pltpu.VMEM((rows, width), BF),
             pltpu.VMEM((slot_rows, part), BF),
-            pltpu.SemaphoreType.DMA((CUTS * per_cut,)),
-            pltpu.SemaphoreType.DMA((per_cut,)),
+            pltpu.SemaphoreType.DMA((2 + CUTS * (part // FINE),)),
+            pltpu.SemaphoreType.DMA((part // FINE,)),
         ],
         compiler_params=room(56),
         cost_estimate=move_cost,
@@ -533,8 +545,15 @@
         tiled=True,
         axis_index_groups=[[2 * i + c for i in range(chips)] for c in range(2)],
     )
-    total = jnp.sum(terms.astype(F32).reshape(chips // 2, 2, 2, latents, STEP), axis=0)
-    return total[:, 0].reshape(2 * latents, STEP), total[:, 1].reshape(2 * latents, STEP)
+    terms = terms.reshape(chips // 2, 2, 2, latents, STEP)
+
+    def summed_over_pairs(grad):
+        total = terms[0, :, grad].astype(F32)
+        for p in range(1, chips // 2):
+            total = total + terms[p, :, grad].astype(F32)
+        return total.reshape(2 * latents, STEP)
+
+    return summed_over_pairs(0), summed_over_pairs(1)
 
 
 def solution(mesh):

time: 164 us -> 163 us (level)
  no operation moved by 1% of the time
where the time goes in v4:
time: 163 us
  waiting for transfers between devices  59.8 us (37%)
  blocking collectives  48.1 us (30%)
  Pallas kernels  27.2 us (17%)
  starting transfers between devices  19.5 us (12%)
  other arithmetic  6.57 us (4%)
    all_to_all x2, waiting for transfers between devices, exchange(): lax.all_to_all(shaped, ('tok', 'lat'), split_axis=0, concat_axis=0, tiled...  52.8 us
    all_to_all x1, blocking collectives, on_device(): lax.all_to_all(summed, 'tok', split_axis=0, concat_axis=0, tiled=True, ax...  19.4 us
    all_to_all x2, starting transfers between devices, exchange(): lax.all_to_all(shaped, ('tok', 'lat'), split_axis=0, concat_axis=0, tiled...  19.3 us
    all_gather x1, blocking collectives, on_device(): loans_a = lax.all_gather(lent_a, 'tok', tiled=True)  15.3 us
    all_gather x1, blocking collectives, on_device(): loans_b = lax.all_gather(lent_b, 'tok', tiled=True)  13.5 us
    pallas_call x1, Pallas kernels, on_device(): mine1, other1 = part_call(scalars, got1, *operands)  8.25 us
    pallas_call x1, Pallas kernels, on_device(): pl.pallas_call(functools.partial(chunk_kernel, True), out_shape=[jax.Shap...  8.03 us
    ppermute x2, waiting for transfers between devices, swap(): return lax.ppermute(values, 'tok', [(i, i ^ 1) for i in range(groups)])  7 us
  transfers between devices with their start and end apart: 4, of which 4 were waited for; matrix products, arithmetic and copies ran while one was open for 2% of the time, Pallas kernels for 9%

profile of v4, /device:TPU:6, one launch (start us, length us, event | category | flops | bytes accessed | tf_op | source)
XLA Modules:
  0.0 162.9 jit_solution(1406449574040968843)
XLA Ops:
  0.6 0.0 copy-start
  0.6 4.0 %first_slots.1 = bf16[512,2048]{1,0:T(8,128)(2,1)} custom-call(s32[1,128]{1,0:T(1,128)} %bitcast.37, s32[1,64]{1,0:T(1,128)} %bitcast.39, bf16[128,8192]{1,0:T(8,128)(2,1)} %tokens_in.1), custom_call_target="tpu_custom_call" | custom-call | flops 1073741824 | bytes 5242880 | tf_op jit(solution)/shard_map/first_slots/pallas_call | solution.py:414
  4.6 0.0 copy-start.1
  4.6 0.0 copy-start.2
  4.6 0.0 copy-start.3
  4.7 13.3 %all-to-all-start.2 = ((bf16[64,8,2048]{2,1,0:T(8,128)(2,1)}), bf16[64,8,2048]{2,1,0:T(8,128)(2,1)}, u32[]{:S(2)}, u32[]{:S(2)}) async-start(bf16[64,8,2048]{2,1,0:T(8,128)(2,1)} %bitcast.41), calls=%async_computation.2 | async-start | bytes 4194304 | tf_op jit(solution)/shard_map/all_to_all | solution.py:443
  18.0 0.0 copy-done.1
  18.0 0.0 copy-done.2
  18.0 0.0 copy-done.3
  18.0 1.1 lent_rows.1
  19.1 15.3 %all_gather.6.loans_a = bf16[448,1024]{1,0:T(8,128)(2,1)S(1)} all-gather(bf16[56,1024]{1,0:T(8,128)(2,1)S(1)} %get-tuple-element.67), channel_id=1, replica_groups=mesh['tok'=8,'lat'=32] {'tok'}, dimensions={0}, use_global_device_ids=true | all-gather | bytes 1032192 | tf_op jit(solution)/shard_map/all_gather | solution.py:453
  34.3 13.5 %all_gather.7.loans_b = bf16[448,1024]{1,0:T(8,128)(2,1)S(1)} all-gather(bf16[56,1024]{1,0:T(8,128)(2,1)S(1)} %get-tuple-element.70), channel_id=1, replica_groups=mesh['tok'=8,'lat'=32] {'tok'}, dimensions={0}, use_global_device_ids=true | all-gather | bytes 1032192 | tf_op jit(solution)/shard_map/all_gather | solution.py:455
  47.8 5.9 %second_slots.1 = (bf16[512,2176]{1,0:T(8,128)(2,1)}, s32[8,128]{1,0:T(8,128)S(1)}) custom-call(s32[1]{0:T(128)} %bitcast.5.group, bf16[128,8192]{1,0:T(8,128)(2,1)S(1)} %copy-done.3, bf16[448,1024]{1,0:T(8,128)(2,1)S(1)} %all_gather.6.loans_a, bf16[448,1024]{1,0:T(8,128)(2,1)S(1)} %all_gather.7.loans_b), custom_call_target="tpu_custom_call" | custom-call | flops 1073741824 | bytes 5242880 | tf_op jit(solution)/shard_map/second_slots/pallas_call | solution.py:457
  53.7 15.5 %all-to-all-done.2 = bf16[64,8,2048]{2,1,0:T(8,128)(2,1)} async-done(((bf16[64,8,2048]{2,1,0:T(8,128)(2,1)}), bf16[64,8,2048]{2,1,0:T(8,128)(2,1)}, u32[]{:S(2)}, u32[]{:S(2)}) %all-to-all-start.2) | async-done | bytes 2097184 | tf_op jit(solution)/shard_map/all_to_all | solution.py:443
  69.3 0.0 copy-start.7
  69.3 6.0 %all-to-all-start.1 = ((bf16[64,8,2176]{2,1,0:T(8,128)(2,1)}), bf16[64,8,2176]{2,1,0:T(8,128)(2,1)}, u32[]{:S(2)}, u32[]{:S(2)}) async-start(bf16[64,8,2176]{2,1,0:T(8,128)(2,1)} %bitcast.8), calls=%async_computation.1 | async-start | bytes 4456448 | tf_op jit(solution)/shard_map/all_to_all | solution.py:443
  75.3 0.0 copy-done
  75.3 0.1 dynamic-slice_bitcast_fusion
  75.4 0.1 copy.17.bias
  75.5 0.1 pad_add_fusion.at
  75.5 0.0 copy-done.7
  75.5 8.2 %chunk_gradients.3 = (f32[4,128,1024]{2,1,0:T(8,128)}, f32[4,128,1024]{2,1,0:T(8,128)}) custom-call(s32[2]{0:T(128)S(1)} %pad_add_fusion.at, bf16[512,2048]{1,0:T(8,128)(2,1)} %bitcast.13.chunk_in, bf16[128,8192]{1,0:T(8,128)(2,1)} %enc_in.3, bf16[128,8192]{1,0:T(8,128)(2,1)} %dec_in.3, f32[64,1]{1,0:T(8,128)S(1)} %copy.17.bias, f32[1,8192]{1,0:T(1,128)S(1)} %bitcast.45), custom_call_target="tpu_custom_call" | custom-call | flops 2684354560 | bytes 12582912 | tf_op jit(solution)/shard_map/chunk_gradients/pallas_call | solution.py:502
  83.8 0.1 collective-permute-start
  83.9 4.4 %collective-permute-done = f32[4,128,1024]{2,1,0:T(8,128)S(1)} collective-permute-done((f32[4,128,1024]{2,1,0:T(8,128)}, f32[4,128,1024]{2,1,0:T(8,128)S(1)}, u32[]{:S(2)}, u32[]{:S(2)}) %collective-permute-start) | collective-permute-done | bytes 2097184 | tf_op jit(solution)/shard_map/ppermute | solution.py:489
  88.3 3.4 %add.126.refs_0_ = f32[4,128,1024]{2,1,0:T(8,128)} add(f32[4,128,1024]{2,1,0:T(8,128)} %get-tuple-element.72, f32[4,128,1024]{2,1,0:T(8,128)S(1)} %collective-permute-done) | non-fusion elementwise | flops 524288 | bytes 6291456 | tf_op jit(solution)/shard_map/add | solution.py:503
  91.6 37.3 %all-to-all-done.1 = bf16[64,8,2176]{2,1,0:T(8,128)(2,1)} async-done(((bf16[64,8,2176]{2,1,0:T(8,128)(2,1)}), bf16[64,8,2176]{2,1,0:T(8,128)(2,1)}, u32[]{:S(2)}, u32[]{:S(2)}) %all-to-all-start.1) | async-done | bytes 2228256 | tf_op jit(solution)/shard_map/all_to_all | solution.py:443
  129.0 8.0 %last_gradients.1 = (f32[4,128,1024]{2,1,0:T(8,128)}, bf16[4,128,1024]{2,1,0:T(8,128)(2,1)S(1)}, f32[1]{0:T(128)}) custom-call(s32[2]{0:T(128)S(1)} %pad_add_fusion.at, bf16[512,2176]{1,0:T(8,128)(2,1)} %bitcast.9.chunk_in, bf16[128,8192]{1,0:T(8,128)(2,1)} %enc_in.3, bf16[128,8192]{1,0:T(8,128)(2,1)} %dec_in.3, f32[64,1]{1,0:T(8,128)S(1)} %copy.17.bias, ...), custom_call_target="tpu_custom_call" | custom-call | flops 2684354560 | bytes 12582912 | tf_op jit(solution)/shard_map/last_gradients/pallas_call | solution.py:504
  137.0 0.7 while.11
  137.6 0.1 collective-permute-start.1
  137.7 2.6 %collective-permute-done.1 = bf16[4,128,1024]{2,1,0:T(8,128)(2,1)S(1)} collective-permute-done((bf16[4,128,1024]{2,1,0:T(8,128)(2,1)S(1)}, bf16[4,128,1024]{2,1,0:T(8,128)(2,1)S(1)}, u32[]{:S(2)}, u32[]{:S(2)}) %collective-permute-start.1) | collective-permute-done | bytes 1048608 | tf_op jit(solution)/shard_map/ppermute | solution.py:489
  140.4 2.0 %add_convert_fusion.1 = bf16[4,128,1024]{2,1,0:T(8,128)(2,1)S(1)} fusion(f32[4,128,1024]{2,1,0:T(8,128)} %get-tuple-element.78, bf16[4,128,1024]{2,1,0:T(8,128)(2,1)S(1)} %collective-permute-done.1), kind=kLoop, calls=%fused_computation.71 | loop fusion | flops 1572864 | bytes 4194304 | tf_op jit(solution)/shard_map/convert_element_type | solution.py:539
  142.4 19.4 %all_to_all.19 = bf16[4,128,1024]{2,1,0:T(8,128)(2,1)S(1)} all-to-all(bf16[4,128,1024]{2,1,0:T(8,128)(2,1)S(1)} %add_convert_fusion.1), channel_id=1, replica_groups={{0,64,128,192},{32,96,160,224},{1,65,129,193},{33,97,161,225},{2,66,130..., dimensions={0} | all-to-all | bytes 2097152 | tf_op jit(solution)/shard_map/all_to_all | solution.py:540
  161.7 1.1 convert_add_fusion
Async XLA Ops:
  0.6 74.6 %copy-start = (f32[128]{0:T(128)S(1)}, f32[128]{0:T(128)}, u32[]{:S(2)}) copy-start(f32[128]{0:T(128)} %param.12) | copy-start | bytes 1540
  4.6 13.4 %copy-start.1 = (s32[128,1]{0,1:T(1,128)S(1)}, s32[128,1]{0,1:T(1,128)}, u32[]{:S(2)}) copy-start(s32[128,1]{0,1:T(1,128)} %param.14) | copy-start | bytes 1540
  4.6 13.4 %copy-start.2 = (s32[64]{0:T(128)S(1)}, s32[64]{0:T(128)}, u32[]{:S(2)}) copy-start(s32[64]{0:T(128)} %param.15) | copy-start | bytes 772
  4.6 13.4 %copy-start.3 = (bf16[128,8192]{1,0:T(8,128)(2,1)S(1)}, bf16[128,8192]{1,0:T(8,128)(2,1)}, u32[]{:S(2)}) copy-start(bf16[128,8192]{1,0:T(8,128)(2,1)} %tokens_in.1) | copy-start | bytes 6291460
  4.7 64.6 %all-to-all-start.2 = ((bf16[64,8,2048]{2,1,0:T(8,128)(2,1)}), bf16[64,8,2048]{2,1,0:T(8,128)(2,1)}, u32[]{:S(2)}, u32[]{:S(2)}) async-start(bf16[64,8,2048]{2,1,0:T(8,128)(2,1)} %bitcast.41), calls=%async_computation.2 | async-start | bytes 4194304 | tf_op jit(solution)/shard_map/all_to_all | solution.py:443
  69.3 6.3 %copy-start.7 = (f32[8192]{0:T(1024)S(1)}, f32[8192]{0:T(1024)}, u32[]{:S(2)}) copy-start(f32[8192]{0:T(1024)} %param.10) | copy-start | bytes 98308
  69.3 59.7 %all-to-all-start.1 = ((bf16[64,8,2176]{2,1,0:T(8,128)(2,1)}), bf16[64,8,2176]{2,1,0:T(8,128)(2,1)}, u32[]{:S(2)}, u32[]{:S(2)}) async-start(bf16[64,8,2176]{2,1,0:T(8,128)(2,1)} %bitcast.8), calls=%async_computation.1 | async-start | bytes 4456448 | tf_op jit(solution)/shard_map/all_to_all | solution.py:443
  83.8 4.5 %collective-permute-start = (f32[4,128,1024]{2,1,0:T(8,128)}, f32[4,128,1024]{2,1,0:T(8,128)S(1)}, u32[]{:S(2)}, u32[]{:S(2)}) collective-permute-start(f32[4,128,1024]{2,1,0:T(8,128)} %get-tuple-element.73), channel_id=1, source_target_pairs={{0,32},{32,0},{64,96},{96,64},{128,160},{160,128},{192,224},{224,1... | collective-permute-start | bytes 6291464 | tf_op jit(solution)/shard_map/ppermute | solution.py:489
  137.6 2.7 %collective-permute-start.1 = (bf16[4,128,1024]{2,1,0:T(8,128)(2,1)S(1)}, bf16[4,128,1024]{2,1,0:T(8,128)(2,1)S(1)}, u32[]{:S(2)}, u32[]{:S(2)}) collective-permute-start(bf16[4,128,1024]{2,1,0:T(8,128)(2,1)S(1)} %get-tuple-element.79), channel_id=1, source_target_pairs={{0,32},{32,0},{64,96},{96,64},{128,160},{160,128},{192,224},{224,1... | collective-permute-start | bytes 3145736 | tf_op jit(solution)/shard_map/ppermute | solution.py:489

commit v5 on v4

--- a/solution.py
+++ b/solution.py
@@ -515,7 +515,8 @@
             pltpu.VMEM(half_shape, F32),
             pltpu.VMEM((slot_rows, EXTRA), BF),
         ],
-        compiler_params=room(56),
+        input_output_aliases={6: 0},
+        compiler_params=room(46),
         cost_estimate=matmul_cost,
         name="last_gradients",
     )(scalars, got2, *operands, prior)

time: 163 us -> 163 us (level)
  no operation moved by 1% of the time
where the time goes in v5:
time: 163 us
  waiting for transfers between devices  59.9 us (37%)
  blocking collectives  48.1 us (30%)
  Pallas kernels  27.1 us (17%)
  starting transfers between devices  19.3 us (12%)
  other arithmetic  6.57 us (4%)
    all_to_all x2, waiting for transfers between devices, exchange(): lax.all_to_all(shaped, ('tok', 'lat'), split_axis=0, concat_axis=0, tiled...  52.9 us
    all_to_all x1, blocking collectives, on_device(): lax.all_to_all(summed, 'tok', split_axis=0, concat_axis=0, tiled=True, ax...  19.4 us
    all_to_all x2, starting transfers between devices, exchange(): lax.all_to_all(shaped, ('tok', 'lat'), split_axis=0, concat_axis=0, tiled...  19.1 us
    all_gather x1, blocking collectives, on_device(): loans_a = lax.all_gather(lent_a, 'tok', tiled=True)  15.3 us
    all_gather x1, blocking collectives, on_device(): loans_b = lax.all_gather(lent_b, 'tok', tiled=True)  13.5 us
    pallas_call x1, Pallas kernels, on_device(): mine1, other1 = part_call(scalars, got1, *operands)  8.27 us
    pallas_call x1, Pallas kernels, on_device(): pl.pallas_call(functools.partial(chunk_kernel, True), out_shape=[jax.Shap...  7.87 us
    ppermute x2, waiting for transfers between devices, swap(): return lax.ppermute(values, 'tok', [(i, i ^ 1) for i in range(groups)])  7 us
  transfers between devices with their start and end apart: 4, of which 4 were waited for; matrix products, arithmetic and copies ran while one was open for 2% of the time, Pallas kernels for 9%

profile of v5, /device:TPU:6, one launch (start us, length us, event | category | flops | bytes accessed | tf_op | source)
XLA Modules:
  0.0 162.8 jit_solution(7051941229718137243)
XLA Ops:
  0.6 0.0 copy-start
  0.6 4.0 %first_slots.1 = bf16[512,2048]{1,0:T(8,128)(2,1)} custom-call(s32[1,128]{1,0:T(1,128)} %bitcast.38, s32[1,64]{1,0:T(1,128)} %bitcast.40, bf16[128,8192]{1,0:T(8,128)(2,1)} %tokens_in.1), custom_call_target="tpu_custom_call" | custom-call | flops 1073741824 | bytes 5242880 | tf_op jit(solution)/shard_map/first_slots/pallas_call | solution.py:414
  4.6 0.0 copy-start.1
  4.6 0.0 copy-start.2
  4.6 0.0 copy-start.5
  4.6 13.3 %all-to-all-start.2 = ((bf16[64,8,2048]{2,1,0:T(8,128)(2,1)}), bf16[64,8,2048]{2,1,0:T(8,128)(2,1)}, u32[]{:S(2)}, u32[]{:S(2)}) async-start(bf16[64,8,2048]{2,1,0:T(8,128)(2,1)} %bitcast.43), calls=%async_computation.2 | async-start | bytes 4194304 | tf_op jit(solution)/shard_map/all_to_all | solution.py:443
  18.0 0.0 copy-done.1
  18.0 0.0 copy-done.2
  18.0 0.0 copy-done.5
  18.0 1.1 lent_rows.1
  19.1 15.3 %all_gather.6.loans_a = bf16[448,1024]{1,0:T(8,128)(2,1)S(1)} all-gather(bf16[56,1024]{1,0:T(8,128)(2,1)S(1)} %get-tuple-element.67), channel_id=1, replica_groups=mesh['tok'=8,'lat'=32] {'tok'}, dimensions={0}, use_global_device_ids=true | all-gather | bytes 1032192 | tf_op jit(solution)/shard_map/all_gather | solution.py:453
  34.3 13.5 %all_gather.7.loans_b = bf16[448,1024]{1,0:T(8,128)(2,1)S(1)} all-gather(bf16[56,1024]{1,0:T(8,128)(2,1)S(1)} %get-tuple-element.70), channel_id=1, replica_groups=mesh['tok'=8,'lat'=32] {'tok'}, dimensions={0}, use_global_device_ids=true | all-gather | bytes 1032192 | tf_op jit(solution)/shard_map/all_gather | solution.py:455
  47.8 5.9 %second_slots.1 = (bf16[512,2176]{1,0:T(8,128)(2,1)}, s32[8,128]{1,0:T(8,128)S(1)}) custom-call(s32[1]{0:T(128)} %bitcast.5.group, bf16[128,8192]{1,0:T(8,128)(2,1)S(1)} %copy-done.5, bf16[448,1024]{1,0:T(8,128)(2,1)S(1)} %all_gather.6.loans_a, bf16[448,1024]{1,0:T(8,128)(2,1)S(1)} %all_gather.7.loans_b), custom_call_target="tpu_custom_call" | custom-call | flops 1073741824 | bytes 5242880 | tf_op jit(solution)/shard_map/second_slots/pallas_call | solution.py:457
  53.7 15.5 %all-to-all-done.2 = bf16[64,8,2048]{2,1,0:T(8,128)(2,1)} async-done(((bf16[64,8,2048]{2,1,0:T(8,128)(2,1)}), bf16[64,8,2048]{2,1,0:T(8,128)(2,1)}, u32[]{:S(2)}, u32[]{:S(2)}) %all-to-all-start.2) | async-done | bytes 2097184 | tf_op jit(solution)/shard_map/all_to_all | solution.py:443
  69.3 0.0 copy-start.9
  69.3 5.8 %all-to-all-start.1 = ((bf16[64,8,2176]{2,1,0:T(8,128)(2,1)}), bf16[64,8,2176]{2,1,0:T(8,128)(2,1)S(1)}, u32[]{:S(2)}, u32[]{:S(2)}) async-start(bf16[64,8,2176]{2,1,0:T(8,128)(2,1)} %bitcast.8), calls=%async_computation.1 | async-start | bytes 4456448 | tf_op jit(solution)/shard_map/all_to_all | solution.py:443
  75.1 0.0 copy-done
  75.1 0.1 dynamic-slice_bitcast_fusion
  75.2 0.1 copy.18.bias
  75.3 0.1 pad_add_fusion.at
  75.4 0.0 copy-done.9
  75.4 8.3 %chunk_gradients.3 = (f32[4,128,1024]{2,1,0:T(8,128)}, f32[4,128,1024]{2,1,0:T(8,128)}) custom-call(s32[2]{0:T(128)S(1)} %pad_add_fusion.at, bf16[512,2048]{1,0:T(8,128)(2,1)} %bitcast.13.chunk_in, bf16[128,8192]{1,0:T(8,128)(2,1)} %enc_in.3, bf16[128,8192]{1,0:T(8,128)(2,1)} %dec_in.3, f32[64,1]{1,0:T(8,128)S(1)} %copy.18.bias, f32[1,8192]{1,0:T(1,128)S(1)} %bitcast.47), custom_call_target="tpu_custom_call" | custom-call | flops 2684354560 | bytes 12582912 | tf_op jit(solution)/shard_map/chunk_gradients/pallas_call | solution.py:502
  83.6 0.1 collective-permute-start
  83.7 4.4 %collective-permute-done = f32[4,128,1024]{2,1,0:T(8,128)S(1)} collective-permute-done((f32[4,128,1024]{2,1,0:T(8,128)}, f32[4,128,1024]{2,1,0:T(8,128)S(1)}, u32[]{:S(2)}, u32[]{:S(2)}) %collective-permute-start) | collective-permute-done | bytes 2097184 | tf_op jit(solution)/shard_map/ppermute | solution.py:489
  88.1 3.4 %add.126.refs_0_ = f32[4,128,1024]{2,1,0:T(8,128)} add(f32[4,128,1024]{2,1,0:T(8,128)} %get-tuple-element.72, f32[4,128,1024]{2,1,0:T(8,128)S(1)} %collective-permute-done) | non-fusion elementwise | flops 524288 | bytes 6291456 | tf_op jit(solution)/shard_map/add | solution.py:503
  91.5 37.3 %all-to-all-done.1 = bf16[64,8,2176]{2,1,0:T(8,128)(2,1)S(1)} async-done(((bf16[64,8,2176]{2,1,0:T(8,128)(2,1)}), bf16[64,8,2176]{2,1,0:T(8,128)(2,1)S(1)}, u32[]{:S(2)}, u32[]{:S(2)}) %all-to-all-start.1) | async-done | bytes 2228256 | tf_op jit(solution)/shard_map/all_to_all | solution.py:443
  128.8 7.9 %last_gradients.1 = (f32[4,128,1024]{2,1,0:T(8,128)}, bf16[4,128,1024]{2,1,0:T(8,128)(2,1)S(1)}, f32[1]{0:T(128)}) custom-call(s32[2]{0:T(128)S(1)} %pad_add_fusion.at, bf16[512,2176]{1,0:T(8,128)(2,1)S(1)} %bitcast.37, bf16[128,8192]{1,0:T(8,128)(2,1)} %enc_in.3, bf16[128,8192]{1,0:T(8,128)(2,1)} %dec_in.3, ...), custom_call_target="tpu_custom_call", output_to_operand_aliasing={{0}: (6, {})} | custom-call | flops 2684354560 | bytes 12582912 | tf_op jit(solution)/shard_map/last_gradients/pallas_call | solution.py:504
  136.7 0.9 while.11
  137.6 0.1 collective-permute-start.1
  137.7 2.6 %collective-permute-done.1 = bf16[4,128,1024]{2,1,0:T(8,128)(2,1)S(1)} collective-permute-done((bf16[4,128,1024]{2,1,0:T(8,128)(2,1)S(1)}, bf16[4,128,1024]{2,1,0:T(8,128)(2,1)S(1)}, u32[]{:S(2)}, u32[]{:S(2)}) %collective-permute-start.1) | collective-permute-done | bytes 1048608 | tf_op jit(solution)/shard_map/ppermute | solution.py:489
  140.3 1.9 %add_convert_fusion.1 = bf16[4,128,1024]{2,1,0:T(8,128)(2,1)S(1)} fusion(f32[4,128,1024]{2,1,0:T(8,128)} %get-tuple-element.78, bf16[4,128,1024]{2,1,0:T(8,128)(2,1)S(1)} %collective-permute-done.1), kind=kLoop, calls=%fused_computation.71 | loop fusion | flops 1572864 | bytes 4194304 | tf_op jit(solution)/shard_map/convert_element_type | solution.py:540
  142.3 19.4 %all_to_all.19 = bf16[4,128,1024]{2,1,0:T(8,128)(2,1)S(1)} all-to-all(bf16[4,128,1024]{2,1,0:T(8,128)(2,1)S(1)} %add_convert_fusion.1), channel_id=1, replica_groups={{0,64,128,192},{32,96,160,224},{1,65,129,193},{33,97,161,225},{2,66,130..., dimensions={0} | all-to-all | bytes 2097152 | tf_op jit(solution)/shard_map/all_to_all | solution.py:541
  161.7 1.1 convert_add_fusion
Async XLA Ops:
  0.6 74.5 %copy-start = (f32[128]{0:T(128)S(1)}, f32[128]{0:T(128)}, u32[]{:S(2)}) copy-start(f32[128]{0:T(128)} %param.12) | copy-start | bytes 1540
  4.6 13.4 %copy-start.1 = (s32[128,1]{0,1:T(1,128)S(1)}, s32[128,1]{0,1:T(1,128)}, u32[]{:S(2)}) copy-start(s32[128,1]{0,1:T(1,128)} %param.14) | copy-start | bytes 1540
  4.6 13.4 %copy-start.2 = (s32[64]{0:T(128)S(1)}, s32[64]{0:T(128)}, u32[]{:S(2)}) copy-start(s32[64]{0:T(128)} %param.15) | copy-start | bytes 772
  4.6 13.4 %copy-start.5 = (bf16[128,8192]{1,0:T(8,128)(2,1)S(1)}, bf16[128,8192]{1,0:T(8,128)(2,1)}, u32[]{:S(2)}) copy-start(bf16[128,8192]{1,0:T(8,128)(2,1)} %tokens_in.1) | copy-start | bytes 6291460
  4.6 64.6 %all-to-all-start.2 = ((bf16[64,8,2048]{2,1,0:T(8,128)(2,1)}), bf16[64,8,2048]{2,1,0:T(8,128)(2,1)}, u32[]{:S(2)}, u32[]{:S(2)}) async-start(bf16[64,8,2048]{2,1,0:T(8,128)(2,1)} %bitcast.43), calls=%async_computation.2 | async-start | bytes 4194304 | tf_op jit(solution)/shard_map/all_to_all | solution.py:443
  69.3 6.1 %copy-start.9 = (f32[8192]{0:T(1024)S(1)}, f32[8192]{0:T(1024)}, u32[]{:S(2)}) copy-start(f32[8192]{0:T(1024)} %param.10) | copy-start | bytes 98308
  69.3 59.6 %all-to-all-start.1 = ((bf16[64,8,2176]{2,1,0:T(8,128)(2,1)}), bf16[64,8,2176]{2,1,0:T(8,128)(2,1)S(1)}, u32[]{:S(2)}, u32[]{:S(2)}) async-start(bf16[64,8,2176]{2,1,0:T(8,128)(2,1)} %bitcast.8), calls=%async_computation.1 | async-start | bytes 4456448 | tf_op jit(solution)/shard_map/all_to_all | solution.py:443
  83.6 4.5 %collective-permute-start = (f32[4,128,1024]{2,1,0:T(8,128)}, f32[4,128,1024]{2,1,0:T(8,128)S(1)}, u32[]{:S(2)}, u32[]{:S(2)}) collective-permute-start(f32[4,128,1024]{2,1,0:T(8,128)} %get-tuple-element.73), channel_id=1, source_target_pairs={{0,32},{32,0},{64,96},{96,64},{128,160},{160,128},{192,224},{224,1... | collective-permute-start | bytes 6291464 | tf_op jit(solution)/shard_map/ppermute | solution.py:489
  137.6 2.7 %collective-permute-start.1 = (bf16[4,128,1024]{2,1,0:T(8,128)(2,1)S(1)}, bf16[4,128,1024]{2,1,0:T(8,128)(2,1)S(1)}, u32[]{:S(2)}, u32[]{:S(2)}) collective-permute-start(bf16[4,128,1024]{2,1,0:T(8,128)(2,1)S(1)} %get-tuple-element.79), channel_id=1, source_target_pairs={{0,32},{32,0},{64,96},{96,64},{128,160},{160,128},{192,224},{224,1... | collective-permute-start | bytes 3145736 | tf_op jit(solution)/shard_map/ppermute | solution.py:489

commit v6 on v5

--- a/solution.py
+++ b/solution.py
@@ -299,7 +299,8 @@
         rows = pl.ds(pl.multiple_of(first_row, latents), latents)
         for i in range(part // STEP):
             here = pl.ds(i * STEP, STEP)
-            self.move(("chunk", i), chunk_in.at[:, here], chunk.at[:, here])
+            if chunk_in is not None:
+                self.move(("chunk", i), chunk_in.at[:, here], chunk.at[:, here])
             for h in range(CUTS):
                 columns = pl.ds(h * part + i * STEP, STEP)
                 self.move(("enc", i, h), enc_in.at[rows, columns], enc.at[:, columns])
@@ -311,7 +312,8 @@
 
     def __call__(self, stage, i):
         if stage == "first":
-            self.moves[("chunk", i)].wait()
+            if ("chunk", i) in self.moves:
+                self.moves[("chunk", i)].wait()
             for h in range(CUTS):
                 self.moves[("enc", i, h)].wait()
         elif stage in self.moves:
@@ -326,11 +328,13 @@
     chunk, enc, dec, cent, err, acc, sems, mine, other, sems_out = refs[:10]
     latents = enc.shape[0]
     core = at[0]
+    received = chunk_in
+    if with_prior:
+        chunk, chunk_in = received.at[:, pl.ds(0, chunk.shape[1])], None
     ready = Loader(sems, at[1], chunk_in, enc_in, dec_in, chunk, enc, dec)
     if with_prior:
-        prior, marks = refs[10:]
+        prior = refs[10]
         ready.move("third", prior_in, prior)
-        ready.move("marks", chunk_in.at[:, pl.ds(chunk.shape[1], EXTRA)], marks)
 
     def out_copy(which, grad):
         source, result = ((mine, mine_out), (other, other_out))[which]
@@ -356,8 +360,7 @@
 
     gradient_body(chunk, enc, dec, bias, dec_bias, cent, err, acc, store, ready)
     if with_prior:
-        ready("marks", 0)
-        flags[0] = jnp.max(marks[...].astype(F32))
+        flags[0] = jnp.max(received[:, chunk.shape[1] :].astype(F32))
     for which in range(2):
         for grad in range(2):
             out_copy(which, grad).wait()
@@ -508,12 +511,11 @@
             jax.ShapeDtypeStruct(half_shape, BF),
             jax.ShapeDtypeStruct((1,), F32),
         ],
-        in_specs=[smem(), anywhere()] + [hbm()] * 2 + [vmem()] * 2 + [hbm()],
+        in_specs=[smem(), vmem()] + [hbm()] * 2 + [vmem()] * 2 + [hbm()],
         out_specs=[anywhere()] * 2 + [smem()],
         scratch_shapes=[
             *work(BF),
             pltpu.VMEM(half_shape, F32),
-            pltpu.VMEM((slot_rows, EXTRA), BF),
         ],
         input_output_aliases={6: 0},
         compiler_params=room(46),

time: 163 us -> 163 us (level)
  no operation moved by 1% of the time
where the time goes in v6:
time: 163 us; the launch traced here: 162 us
  waiting for transfers between devices  59.9 us (37%)
  blocking collectives  48.1 us (30%)
  Pallas kernels  26.9 us (17%)
  starting transfers between devices  19.3 us (12%)
  other arithmetic  6.57 us (4%)
    all_to_all x2, waiting for transfers between devices, exchange(): lax.all_to_all(shaped, ('tok', 'lat'), split_axis=0, concat_axis=0, tiled...  52.9 us
    all_to_all x1, blocking collectives, on_device(): lax.all_to_all(summed, 'tok', split_axis=0, concat_axis=0, tiled=True, ax...  19.4 us
    all_to_all x2, starting transfers between devices, exchange(): lax.all_to_all(shaped, ('tok', 'lat'), split_axis=0, concat_axis=0, tiled...  19.1 us
    all_gather x1, blocking collectives, on_device(): loans_a = lax.all_gather(lent_a, 'tok', tiled=True)  15.3 us
    all_gather x1, blocking collectives, on_device(): loans_b = lax.all_gather(lent_b, 'tok', tiled=True)  13.5 us
    pallas_call x1, Pallas kernels, on_device(): mine1, other1 = part_call(scalars, got1, *operands)  8.27 us
    pallas_call x1, Pallas kernels, on_device(): pl.pallas_call(functools.partial(chunk_kernel, True), out_shape=[jax.Shap...  7.72 us
    ppermute x2, waiting for transfers between devices, swap(): return lax.ppermute(values, 'tok', [(i, i ^ 1) for i in range(groups)])  7 us
  transfers between devices with their start and end apart: 4, of which 4 were waited for; matrix products, arithmetic and copies ran while one was open for 2% of the time, Pallas kernels for 9%

profile of v6, /device:TPU:6, one launch (start us, length us, event | category | flops | bytes accessed | tf_op | source)
XLA Modules:
  0.0 162.4 jit_solution(6807564555275923593)
XLA Ops:
  0.6 0.0 copy-start
  0.6 4.0 %first_slots.1 = bf16[512,2048]{1,0:T(8,128)(2,1)} custom-call(s32[1,128]{1,0:T(1,128)} %bitcast.38, s32[1,64]{1,0:T(1,128)} %bitcast.40, bf16[128,8192]{1,0:T(8,128)(2,1)} %tokens_in.1), custom_call_target="tpu_custom_call" | custom-call | flops 1073741824 | bytes 5242880 | tf_op jit(solution)/shard_map/first_slots/pallas_call | solution.py:417
  4.6 0.0 copy-start.1
  4.6 0.0 copy-start.2
  4.6 0.0 copy-start.5
  4.6 13.3 %all-to-all-start.2 = ((bf16[64,8,2048]{2,1,0:T(8,128)(2,1)}), bf16[64,8,2048]{2,1,0:T(8,128)(2,1)}, u32[]{:S(2)}, u32[]{:S(2)}) async-start(bf16[64,8,2048]{2,1,0:T(8,128)(2,1)} %bitcast.43), calls=%async_computation.2 | async-start | bytes 4194304 | tf_op jit(solution)/shard_map/all_to_all | solution.py:446
  18.0 0.0 copy-done.1
  18.0 0.0 copy-done.2
  18.0 0.0 copy-done.5
  18.0 1.1 lent_rows.1
  19.1 15.3 %all_gather.6.loans_a = bf16[448,1024]{1,0:T(8,128)(2,1)S(1)} all-gather(bf16[56,1024]{1,0:T(8,128)(2,1)S(1)} %get-tuple-element.67), channel_id=1, replica_groups=mesh['tok'=8,'lat'=32] {'tok'}, dimensions={0}, use_global_device_ids=true | all-gather | bytes 1032192 | tf_op jit(solution)/shard_map/all_gather | solution.py:456
  34.3 13.5 %all_gather.7.loans_b = bf16[448,1024]{1,0:T(8,128)(2,1)S(1)} all-gather(bf16[56,1024]{1,0:T(8,128)(2,1)S(1)} %get-tuple-element.70), channel_id=1, replica_groups=mesh['tok'=8,'lat'=32] {'tok'}, dimensions={0}, use_global_device_ids=true | all-gather | bytes 1032192 | tf_op jit(solution)/shard_map/all_gather | solution.py:458
  47.8 5.9 %second_slots.1 = (bf16[512,2176]{1,0:T(8,128)(2,1)}, s32[8,128]{1,0:T(8,128)S(1)}) custom-call(s32[1]{0:T(128)} %bitcast.5.group, bf16[128,8192]{1,0:T(8,128)(2,1)S(1)} %copy-done.5, bf16[448,1024]{1,0:T(8,128)(2,1)S(1)} %all_gather.6.loans_a, bf16[448,1024]{1,0:T(8,128)(2,1)S(1)} %all_gather.7.loans_b), custom_call_target="tpu_custom_call" | custom-call | flops 1073741824 | bytes 5242880 | tf_op jit(solution)/shard_map/second_slots/pallas_call | solution.py:460
  53.7 15.5 %all-to-all-done.2 = bf16[64,8,2048]{2,1,0:T(8,128)(2,1)} async-done(((bf16[64,8,2048]{2,1,0:T(8,128)(2,1)}), bf16[64,8,2048]{2,1,0:T(8,128)(2,1)}, u32[]{:S(2)}, u32[]{:S(2)}) %all-to-all-start.2) | async-done | bytes 2097184 | tf_op jit(solution)/shard_map/all_to_all | solution.py:446
  69.3 0.0 copy-start.9
  69.3 5.8 %all-to-all-start.1 = ((bf16[64,8,2176]{2,1,0:T(8,128)(2,1)}), bf16[64,8,2176]{2,1,0:T(8,128)(2,1)S(1)}, u32[]{:S(2)}, u32[]{:S(2)}) async-start(bf16[64,8,2176]{2,1,0:T(8,128)(2,1)} %bitcast.8), calls=%async_computation.1 | async-start | bytes 4456448 | tf_op jit(solution)/shard_map/all_to_all | solution.py:446
  75.1 0.0 copy-done
  75.1 0.1 dynamic-slice_bitcast_fusion
  75.2 0.1 copy.18.bias
  75.3 0.1 pad_add_fusion.at
  75.4 0.0 copy-done.9
  75.4 8.3 %chunk_gradients.3 = (f32[4,128,1024]{2,1,0:T(8,128)}, f32[4,128,1024]{2,1,0:T(8,128)}) custom-call(s32[2]{0:T(128)S(1)} %pad_add_fusion.at, bf16[512,2048]{1,0:T(8,128)(2,1)} %bitcast.13.chunk_in, bf16[128,8192]{1,0:T(8,128)(2,1)} %enc_in.3, bf16[128,8192]{1,0:T(8,128)(2,1)} %dec_in.3, f32[64,1]{1,0:T(8,128)S(1)} %copy.18.bias, f32[1,8192]{1,0:T(1,128)S(1)} %bitcast.47), custom_call_target="tpu_custom_call" | custom-call | flops 2684354560 | bytes 12582912 | tf_op jit(solution)/shard_map/chunk_gradients/pallas_call | solution.py:505
  83.6 0.1 collective-permute-start
  83.7 4.4 %collective-permute-done = f32[4,128,1024]{2,1,0:T(8,128)S(1)} collective-permute-done((f32[4,128,1024]{2,1,0:T(8,128)}, f32[4,128,1024]{2,1,0:T(8,128)S(1)}, u32[]{:S(2)}, u32[]{:S(2)}) %collective-permute-start) | collective-permute-done | bytes 2097184 | tf_op jit(solution)/shard_map/ppermute | solution.py:492
  88.1 3.4 %add.126.refs_0_ = f32[4,128,1024]{2,1,0:T(8,128)} add(f32[4,128,1024]{2,1,0:T(8,128)} %get-tuple-element.72, f32[4,128,1024]{2,1,0:T(8,128)S(1)} %collective-permute-done) | non-fusion elementwise | flops 524288 | bytes 6291456 | tf_op jit(solution)/shard_map/add | solution.py:506
  91.5 37.3 %all-to-all-done.1 = bf16[64,8,2176]{2,1,0:T(8,128)(2,1)S(1)} async-done(((bf16[64,8,2176]{2,1,0:T(8,128)(2,1)}), bf16[64,8,2176]{2,1,0:T(8,128)(2,1)S(1)}, u32[]{:S(2)}, u32[]{:S(2)}) %all-to-all-start.1) | async-done | bytes 2228256 | tf_op jit(solution)/shard_map/all_to_all | solution.py:446
  128.8 7.7 %last_gradients.1 = (f32[4,128,1024]{2,1,0:T(8,128)}, bf16[4,128,1024]{2,1,0:T(8,128)(2,1)S(1)}, f32[1]{0:T(128)}) custom-call(s32[2]{0:T(128)S(1)} %pad_add_fusion.at, bf16[512,2176]{1,0:T(8,128)(2,1)S(1)} %bitcast.37, bf16[128,8192]{1,0:T(8,128)(2,1)} %enc_in.3, bf16[128,8192]{1,0:T(8,128)(2,1)} %dec_in.3, ...), custom_call_target="tpu_custom_call", output_to_operand_aliasing={{0}: (6, {})} | custom-call | flops 2684354560 | bytes 12582912 | tf_op jit(solution)/shard_map/last_gradients/pallas_call | solution.py:507
  136.6 0.7 while.11
  137.2 0.1 collective-permute-start.1
  137.3 2.6 %collective-permute-done.1 = bf16[4,128,1024]{2,1,0:T(8,128)(2,1)S(1)} collective-permute-done((bf16[4,128,1024]{2,1,0:T(8,128)(2,1)S(1)}, bf16[4,128,1024]{2,1,0:T(8,128)(2,1)S(1)}, u32[]{:S(2)}, u32[]{:S(2)}) %collective-permute-start.1) | collective-permute-done | bytes 1048608 | tf_op jit(solution)/shard_map/ppermute | solution.py:492
  140.0 1.9 %add_convert_fusion.1 = bf16[4,128,1024]{2,1,0:T(8,128)(2,1)S(1)} fusion(f32[4,128,1024]{2,1,0:T(8,128)} %get-tuple-element.78, bf16[4,128,1024]{2,1,0:T(8,128)(2,1)S(1)} %collective-permute-done.1), kind=kLoop, calls=%fused_computation.71 | loop fusion | flops 1572864 | bytes 4194304 | tf_op jit(solution)/shard_map/convert_element_type | solution.py:542
  141.9 19.4 %all_to_all.19 = bf16[4,128,1024]{2,1,0:T(8,128)(2,1)S(1)} all-to-all(bf16[4,128,1024]{2,1,0:T(8,128)(2,1)S(1)} %add_convert_fusion.1), channel_id=1, replica_groups={{0,64,128,192},{32,96,160,224},{1,65,129,193},{33,97,161,225},{2,66,130..., dimensions={0} | all-to-all | bytes 2097152 | tf_op jit(solution)/shard_map/all_to_all | solution.py:543
  161.3 1.1 convert_add_fusion
Async XLA Ops:
  0.6 74.5 %copy-start = (f32[128]{0:T(128)S(1)}, f32[128]{0:T(128)}, u32[]{:S(2)}) copy-start(f32[128]{0:T(128)} %param.12) | copy-start | bytes 1540
  4.6 13.4 %copy-start.1 = (s32[128,1]{0,1:T(1,128)S(1)}, s32[128,1]{0,1:T(1,128)}, u32[]{:S(2)}) copy-start(s32[128,1]{0,1:T(1,128)} %param.14) | copy-start | bytes 1540
  4.6 13.4 %copy-start.2 = (s32[64]{0:T(128)S(1)}, s32[64]{0:T(128)}, u32[]{:S(2)}) copy-start(s32[64]{0:T(128)} %param.15) | copy-start | bytes 772
  4.6 13.4 %copy-start.5 = (bf16[128,8192]{1,0:T(8,128)(2,1)S(1)}, bf16[128,8192]{1,0:T(8,128)(2,1)}, u32[]{:S(2)}) copy-start(bf16[128,8192]{1,0:T(8,128)(2,1)} %tokens_in.1) | copy-start | bytes 6291460
  4.6 64.6 %all-to-all-start.2 = ((bf16[64,8,2048]{2,1,0:T(8,128)(2,1)}), bf16[64,8,2048]{2,1,0:T(8,128)(2,1)}, u32[]{:S(2)}, u32[]{:S(2)}) async-start(bf16[64,8,2048]{2,1,0:T(8,128)(2,1)} %bitcast.43), calls=%async_computation.2 | async-start | bytes 4194304 | tf_op jit(solution)/shard_map/all_to_all | solution.py:446
  69.3 6.1 %copy-start.9 = (f32[8192]{0:T(1024)S(1)}, f32[8192]{0:T(1024)}, u32[]{:S(2)}) copy-start(f32[8192]{0:T(1024)} %param.10) | copy-start | bytes 98308
  69.3 59.6 %all-to-all-start.1 = ((bf16[64,8,2176]{2,1,0:T(8,128)(2,1)}), bf16[64,8,2176]{2,1,0:T(8,128)(2,1)S(1)}, u32[]{:S(2)}, u32[]{:S(2)}) async-start(bf16[64,8,2176]{2,1,0:T(8,128)(2,1)} %bitcast.8), calls=%async_computation.1 | async-start | bytes 4456448 | tf_op jit(solution)/shard_map/all_to_all | solution.py:446
  83.6 4.5 %collective-permute-start = (f32[4,128,1024]{2,1,0:T(8,128)}, f32[4,128,1024]{2,1,0:T(8,128)S(1)}, u32[]{:S(2)}, u32[]{:S(2)}) collective-permute-start(f32[4,128,1024]{2,1,0:T(8,128)} %get-tuple-element.73), channel_id=1, source_target_pairs={{0,32},{32,0},{64,96},{96,64},{128,160},{160,128},{192,224},{224,1... | collective-permute-start | bytes 6291464 | tf_op jit(solution)/shard_map/ppermute | solution.py:492
  137.2 2.7 %collective-permute-start.1 = (bf16[4,128,1024]{2,1,0:T(8,128)(2,1)S(1)}, bf16[4,128,1024]{2,1,0:T(8,128)(2,1)S(1)}, u32[]{:S(2)}, u32[]{:S(2)}) collective-permute-start(bf16[4,128,1024]{2,1,0:T(8,128)(2,1)S(1)} %get-tuple-element.79), channel_id=1, source_target_pairs={{0,32},{32,0},{64,96},{96,64},{128,160},{160,128},{192,224},{224,1... | collective-permute-start | bytes 3145736 | tf_op jit(solution)/shard_map/ppermute | solution.py:492
